TPU v7x, 32 devices: a whole 2x2x4 slice. The times are simulated.
32 devices in a mesh: groups: 2 (over x), sink: 16 (over z, y, core).
Axes of the slice: x: 2, y: 2, z: 4, core: 2. Of those that a mesh axis runs over, the one named last changes fastest.
Arguments:
- blocks: bfloat16 [4096, 128, 128], P(('groups', 'sink')), parts along dimension 0, may hold values from -6 to 6
- peram: bfloat16 [256, 4, 16, 128], P(('groups', 'sink')), parts along dimension 0, may hold values from -0.5 to 0.5
- src_blocks: bfloat16 [256, 2, 128, 128], P(('groups', 'sink')), parts along dimension 0, may hold values from -1 to 1
- sink_spin: int32 [16, 3], replicated, may hold values from 0 to 3
- src_spin: int32 [1, 3], replicated, may hold values from 0 to 3
- pairs: int32 [4, 2], replicated, may hold values from 0 to 3
Outputs:
- transformed: bfloat16 [256, 16, 128, 128], P(('groups', 'sink')), parts along dimension 0
- correlator: float32 [2, 4, 4], P('groups'), parts along dimension 0
There are 2 independent parts, one for each index of `groups`. A program takes and returns all parts, laid end to end along the dimension named above; an argument that names none is the same for every part. Nothing has to cross between parts.
All inputs are finite; a program needn't handle non-finite values.
Results may differ from a plain program's by a relative error of at most 0.0087.
Values may be sent and summed in bfloat16 or wider, within the bound.
No kernel may reach another device: no remote copies, remote signals or barrier semaphores. Data moves between devices by JAX's collectives and lax.ppermute only.
A program may use at most 64 MiB of HBM per device.

v0:
```python
import jax
import jax.numpy as jnp
from jax import lax
from jax.sharding import PartitionSpec as P

NMOM = 4


def mode_last(cube, factor):
    width = cube.shape[0]
    flat = jnp.dot(cube.reshape(width * width, width), factor, preferred_element_type=jnp.float32)
    return flat.reshape(width, width, width).astype(jnp.bfloat16)


def mode_middle(inner, factor):
    return jnp.einsum("ijk,jJ->iJk", inner, factor, preferred_element_type=jnp.float32).astype(
        jnp.bfloat16
    )


def mode_first(inner, factor):
    return jnp.einsum("iI,iJk->IJk", factor, inner, preferred_element_type=jnp.float32).astype(
        jnp.bfloat16
    )


def body(blocks, peram, src_blocks, sink_spin, src_spin, pairs):
    width = blocks.shape[1]
    tsources = src_spin.shape[0]
    devices = lax.axis_size("sink")
    position = lax.axis_index("sink")
    per_rows = peram.shape[0]
    own_rows = position * per_rows + jnp.arange(per_rows, dtype=jnp.int32)
    own_source = own_rows // width
    targets = jnp.arange(devices, dtype=jnp.int32)
    target_time = targets // NMOM
    codes = 4 * sink_spin[None, :, :] + src_spin[own_source][:, None, :]
    picked = peram[
        jnp.arange(per_rows, dtype=jnp.int32)[:, None, None], target_time[None, :, None], codes, :
    ]
    incoming = lax.all_to_all(picked, "sink", split_axis=1, concat_axis=0, tiled=True)
    factors = incoming.reshape(tsources, width, 3, width)
    middles = mode_middle(mode_last(blocks, factors[0, :, 2, :]), factors[0, :, 1, :])
    finished = jnp.stack([mode_first(middles, factors[0, :, 0, :])])
    sending = finished.reshape(tsources * width, 1, width, width)
    regrouped = lax.all_to_all(sending, "sink", split_axis=0, concat_axis=1, tiled=True)
    out_rows = regrouped.shape[0]
    row_index = position * out_rows + jnp.arange(out_rows, dtype=jnp.int32)
    row_source = row_index // width
    partial_sums = jnp.einsum(
        "rbjk,rcjk->rbc", regrouped, src_blocks, preferred_element_type=jnp.float32
    )
    selector = (row_source[:, None] == jnp.arange(tsources, dtype=jnp.int32)[None, :]).astype(
        jnp.float32
    )
    local_correlation = jnp.einsum(
        "rs,rbc->sbc", selector, partial_sums, precision=lax.Precision.HIGHEST
    )
    correlation = lax.psum(local_correlation, "sink")
    ncount = src_blocks.shape[1]
    grid = correlation.reshape(tsources, devices // NMOM, NMOM, ncount)
    momenta = jnp.arange(NMOM, dtype=jnp.int32)
    pick_first = (pairs[:, 0][:, None] == momenta[None, :]).astype(jnp.float32)
    pick_second = (pairs[:, 1][:, None] == momenta[None, :]).astype(jnp.float32)
    first_one = jnp.einsum("pm,stmc->stpc", pick_first, grid, precision=lax.Precision.HIGHEST)
    second_one = jnp.einsum("pm,stmc->stpc", pick_second, grid, precision=lax.Precision.HIGHEST)
    correlator = first_one[..., 0] * second_one[..., 1] - first_one[..., 1] * second_one[..., 0]
    return (regrouped, correlator)


def solution(mesh):
    placed = (
        P(("groups", "sink"), None, None),
        P(("groups", "sink"), None, None, None),
        P(("groups", "sink"), None, None, None),
        P(),
        P(),
        P(),
    )
    return jax.shard_map(
        body,
        mesh=mesh,
        in_specs=placed,
        out_specs=(P(("groups", "sink"), None, None, None), P("groups", None, None)),
        check_vma=False,
    )
```

profile of v0, /device:TPU:0, one launch (start us, length us, event | category | flops | bytes accessed | tf_op | source)
XLA Modules:
  0.0 188.6 jit_solution(2369113357062948209)
XLA Ops:
  0.6 0.0 copy-start
  0.7 0.7 broadcast_multiply_fusion
  1.4 0.1 copy.31
  1.5 0.7 fusion.14
  2.2 0.2 reshape.165
  2.4 6.9 %gather_fusion = bf16[384,128]{1,0:T(8,128)(2,1)S(1)} fusion(bf16[8,4,16,128]{3,2,1,0:T(8,128)(2,1)} %param.7, s32[384]{0:T(512)S(1)} %reshape.165), kind=kCustom, calls=%fused_computation | custom fusion | bytes 201216 | tf_op jit(solution)/shard_map/gather | solution.py:38
  9.3 0.1 reshape.168
  9.3 0.1 copy.32
  9.4 14.6 %all_to_all.33 = bf16[8,16,3,128]{3,0,2,1:T(8,128)(2,1)S(1)} all-to-all(bf16[8,16,3,128]{3,0,2,1:T(8,128)(2,1)S(1)} %copy.32), channel_id=1, replica_groups=mesh['groups'=2,'sink'=16] {'sink'}, dimensions={1} | all-to-all | bytes 196608 | tf_op jit(solution)/shard_map/all_to_all | solution.py:41
  24.1 5.5 %fusion = bf16[16384,128]{0,1:T(8,128)(2,1)} fusion(bf16[16384,128]{1,0:T(8,128)(2,1)} %bitcast.78, bf16[1,128,3,128]{3,1,2,0:T(8,128)(2,1)S(1)} %bitcast.79), kind=kOutput, calls=%fused_computation.2 | convolution fusion | flops 538968064 | bytes 8421376 | tf_op jit(solution)/shard_map/dot_general | solution.py:11
  29.5 6.4 %copy.50 = bf16[16384,128]{1,0:T(8,128)(2,1)} copy(bf16[16384,128]{0,1:T(8,128)(2,1)} %fusion) | data formatting | bytes 8388608 | tf_op jit(solution)/shard_map/convert_element_type | solution.py:12
  35.9 3.5 %convert_bitcast_fusion.1 = bf16[128,128,128]{2,1,0:T(8,128)(2,1)S(1)} fusion(bf16[128,128,128]{2,1,0:T(8,128)(2,1)} %bitcast.77, bf16[1,128,3,128]{3,1,2,0:T(8,128)(2,1)S(1)} %bitcast.80), kind=kOutput, calls=%fused_computation.9 | convolution fusion | flops 538968064 | bytes 8421376 | tf_op jit(solution)/shard_map/ijk,jJ->iJk/dot_general | solution.py:16
  39.4 3.4 %convert_bitcast_fusion = bf16[128,1,128,128]{3,0,2,1:T(8,128)(2,1)S(1)} fusion(bf16[128,128,128]{2,1,0:T(8,128)(2,1)S(1)} %convert_bitcast_fusion.1, bf16[1,128,3,128]{3,1,2,0:T(8,128)(2,1)S(1)} %bitcast.81), kind=kOutput, calls=%fused_computation.8 | convolution fusion | flops 538968064 | bytes 8421376 | tf_op jit(solution)/shard_map/iI,iJk->IJk/dot_general | solution.py:22
  42.8 4.7 %copy.38 = bf16[128,1,128,128]{3,2,1,0:T(8,128)(2,1)} copy(bf16[128,1,128,128]{3,0,2,1:T(8,128)(2,1)S(1)} %convert_bitcast_fusion) | data formatting | bytes 8388608 | tf_op jit(solution)/shard_map/reshape;stack | solution.py:45
  47.5 0.0 copy-start.1
  47.5 4.8 %all-to-all-start.1 = ((bf16[128,1,128,128]{3,2,1,0:T(8,128)(2,1)}), bf16[128,1,128,128]{3,2,1,0:T(8,128)(2,1)}, u32[]{:S(2)}, u32[]{:S(2)}) async-start(bf16[128,1,128,128]{3,2,1,0:T(8,128)(2,1)} %copy.38), calls=%async_computation.1 | async-start | bytes 8388608 | tf_op jit(solution)/shard_map/all_to_all | solution.py:46
  52.4 0.0 copy-done.1
  52.4 77.6 %all-to-all-done.1 = bf16[128,1,128,128]{3,2,1,0:T(8,128)(2,1)} async-done(((bf16[128,1,128,128]{3,2,1,0:T(8,128)(2,1)}), bf16[128,1,128,128]{3,2,1,0:T(8,128)(2,1)}, u32[]{:S(2)}, u32[]{:S(2)}) %all-to-all-start.1) | async-done | bytes 4194336 | tf_op jit(solution)/shard_map/all_to_all | solution.py:46
  129.9 0.0 copy-done
  130.0 5.0 %fusion.8 = f32[8,16,2]{1,2,0:T(2,128)S(1)} fusion(bf16[16,8,1,128,128]{4,3,1,0,2:T(8,128)(2,1)} %bitcast.16, bf16[8,2,128,128]{3,2,1,0:T(8,128)(2,1)S(1)} %copy-done), kind=kOutput, calls=%fused_computation.10 | convolution fusion | flops 8388608 | bytes 4719616 | tf_op jit(solution)/shard_map/rbjk,rcjk->rbc/dot_general | solution.py:50
  135.0 0.1 fusion.15
  135.1 0.1 reshape.162
  135.2 47.6 %psum.7 = f32[4,4,2]{1,0,2:T(4,128)S(1)} all-reduce(f32[4,4,2]{1,0,2:T(4,128)S(1)} %reshape.162), channel_id=1, replica_groups=mesh['groups'=2,'sink'=16] {'sink'}, use_global_device_ids=true, to_apply=%region_0.1 | all-reduce | flops 32 | bytes 256 | tf_op jit(solution)/shard_map/psum | solution.py:59
  182.8 0.2 convolution_bitcast_fusion
  183.0 0.2 convolution_bitcast_fusion.1
  183.2 4.8 %copy.43 = bf16[8,16,128,128]{3,2,1,0:T(8,128)(2,1)} copy(bf16[8,16,128,128]{3,2,0,1:T(8,128)(2,1)} %bitcast.19) | data formatting | bytes 8388608
  188.0 0.6 fusion.19
  (3 shorter events, 0.0 us)
Async XLA Ops:
  0.6 129.3 %copy-start = (bf16[8,2,128,128]{3,2,1,0:T(8,128)(2,1)S(1)}, bf16[8,2,128,128]{3,2,1,0:T(8,128)(2,1)}, u32[]{:S(2)}) copy-start(bf16[8,2,128,128]{3,2,1,0:T(8,128)(2,1)} %param.8) | copy-start | bytes 1572868
  47.5 4.9 %copy-start.1 = (s32[4,2]{0,1:T(2,128)S(1)}, s32[4,2]{0,1:T(2,128)}, u32[]{:S(2)}) copy-start(s32[4,2]{0,1:T(2,128)} %param.11) | copy-start | bytes 100
  47.5 82.4 %all-to-all-start.1 = ((bf16[128,1,128,128]{3,2,1,0:T(8,128)(2,1)}), bf16[128,1,128,128]{3,2,1,0:T(8,128)(2,1)}, u32[]{:S(2)}, u32[]{:S(2)}) async-start(bf16[128,1,128,128]{3,2,1,0:T(8,128)(2,1)} %copy.38), calls=%async_computation.1 | async-start | bytes 8388608 | tf_op jit(solution)/shard_map/all_to_all | solution.py:46
where the time goes:
time: 189 us
  waiting for transfers between devices  77.6 us (41%)
  blocking collectives  62.2 us (33%)
  local copies, waits for them, and re-layouts  23.3 us (12%)
  matrix products  17.9 us (9%)
  starting transfers between devices  4.84 us (3%)
  other arithmetic  2.06 us (1%)
    all_to_all x1, waiting for transfers between devices, body(): lax.all_to_all(sending, 'sink', split_axis=0, concat_axis=1, tiled=True)  77.6 us
    psum x1, blocking collectives, body(): correlation = lax.psum(local_correlation, 'sink')  47.6 us
    all_to_all x1, blocking collectives, body(): lax.all_to_all(picked, 'sink', split_axis=1, concat_axis=0, tiled=True)  14.6 us
    gather x3, local copies, waits for them, and re-layouts, body(): peram[jnp.arange(per_rows, dtype=jnp.int32)[:, None, None], target_time[N...  7 us
    convert_element_type x1, local copies, waits for them, and re-layouts, mode_last(): return flat.reshape(width, width, width).astype(jnp.bfloat16)  6.39 us
    dot_general x1, matrix products, mode_last(): jnp.dot(cube.reshape(width * width, width), factor, preferred_element_typ...  5.48 us
    dot_general x1, matrix products, body(): jnp.einsum('rbjk,rcjk->rbc', regrouped, src_blocks, preferred_element_typ...  5 us
    all_to_all x1, starting transfers between devices, body(): lax.all_to_all(sending, 'sink', split_axis=0, concat_axis=1, tiled=True)  4.84 us
  transfers between devices with their start and end apart: 1, of which 1 were waited for; matrix products, arithmetic and copies ran while one was open for 0% of the time, Pallas kernels for 0%

commit v1 on v0

v1 whole, which is shorter than its diff:
```python
import jax
import jax.numpy as jnp
from jax import lax
from jax.experimental import pallas as pl
from jax.experimental.pallas import tpu as pltpu
from jax.sharding import PartitionSpec as P

NMOM = 4
PITCH = 136
GROUP = 16
F32 = jnp.float32
BF16 = jnp.bfloat16
IN_VMEM = pl.BlockSpec(memory_space=pltpu.VMEM)
IN_SMEM = pl.BlockSpec(memory_space=pltpu.SMEM)
IN_HBM = pl.BlockSpec(memory_space=pltpu.HBM)
AHEAD = 5


def in_hbm(array):
    return pltpu.with_memory_space_constraint(array, pltpu.HBM)


def in_vmem(array):
    return pltpu.with_memory_space_constraint(array, pltpu.VMEM)


def dot(left, right):
    return jnp.dot(left, right, preferred_element_type=F32)


def pick_kernel(sink_spin, src_spin, peram, out, table):
    times, codes = peram.shape[1:3]
    for t in range(times):
        table[pl.ds(t * codes, codes)] = jnp.swapaxes(peram[:, t].astype(F32), 0, 1)
    for b in range(out.shape[0]):
        for m in range(3):
            code = (b // NMOM) * codes + 4 * sink_spin[m, b] + src_spin[0, m]
            out[b, m] = table[code].astype(BF16)


def pick(peram, sink_spin, src_spin):
    rows, times, codes, width = peram.shape
    blocks = sink_spin.shape[0]
    return pl.pallas_call(
        pick_kernel,
        out_shape=jax.ShapeDtypeStruct((blocks, 3, rows, width), BF16),
        in_specs=[IN_SMEM, IN_SMEM, IN_VMEM],
        out_specs=IN_VMEM,
        scratch_shapes=[pltpu.VMEM((times * codes, rows, width), F32)],
        name="pick",
    )(sink_spin.T, src_spin, peram)


def contract(me, blocks, factors, classes):
    width = blocks.shape[0]
    rows = factors.shape[2]
    half = width // 2
    steps = half // GROUP

    def kernel(me, blocks, factors, *refs):
        outs, (left0, wide2, second, held, kept, sems) = refs[: len(classes)], refs[len(classes) :]
        made = [kept.at[q - AHEAD] if q >= AHEAD else out for q, out in enumerate(outs)]
        copies = []
        for step in range(steps):
            part = pl.ds(step * 2 * GROUP, 2 * GROUP)
            copies.append(pltpu.make_async_copy(blocks.at[part], held.at[part], sems.at[step]))
            copies[-1].start()
        parts = [factors[:, m].astype(F32).reshape(width, width) for m in range(3)]
        left1 = parts[1].T.astype(BF16)
        left0[...] = parts[0].T
        zero = jnp.zeros((width, width), BF16)
        right2 = parts[2].astype(BF16)
        wide2[...] = jnp.concatenate(
            [jnp.concatenate([right2, zero], 1), jnp.concatenate([zero, right2], 1)], 0
        )

        for step in range(steps):
            copies[step].wait()
            base = step * 2 * GROUP
            pairs = [
                jnp.concatenate([held[base + 2 * q], held[base + 2 * q + 1]], 1)
                for q in range(GROUP)
            ]
            first = dot(jnp.concatenate(pairs, 0), wide2[...]).astype(BF16)
            for q in range(GROUP):
                done = dot(left1, first[q * width : (q + 1) * width]).astype(BF16).astype(F32)
                for h in range(2):
                    start = (base + 2 * q + h) * PITCH
                    second[pl.ds(start, width), :] = done[:, h * width : (h + 1) * width]
        left = jnp.concatenate(
            [left0[pl.ds(pl.multiple_of((me[0] ^ d) * rows, rows), rows), :] for d in classes], 0
        ).astype(BF16)

        for step in range(steps):
            base = step * 2 * GROUP
            done = []
            for q in range(GROUP):
                right = jnp.concatenate(
                    [
                        second[pl.ds(base + 2 * q + h, width, stride=PITCH), :].astype(BF16)
                        for h in range(2)
                    ],
                    1,
                )
                done.append(dot(left, right))
            for index in range(len(classes)):
                tiles = []
                for q in range(GROUP):
                    own = done[q][index * rows : (index + 1) * rows]
                    tiles += [own[:, :width], own[:, width:]]
                part = pl.ds(base * rows, 2 * GROUP * rows)
                made[index][part, :] = jnp.concatenate(tiles, 0).astype(BF16)
            for index in range(AHEAD, len(classes)):
                copies.append(
                    pltpu.make_async_copy(
                        made[index].at[part], outs[index].at[part], sems.at[len(copies)]
                    )
                )
                copies[-1].start()
        for copy in copies[steps:]:
            copy.wait()

    flops = 2 * 3 * width**4
    return pl.pallas_call(
        kernel,
        out_shape=[pltpu.VMEM((width * rows, width), BF16)] * AHEAD
        + [pltpu.HBM((width * rows, width), BF16)] * (len(classes) - AHEAD),
        in_specs=[IN_SMEM, IN_HBM, IN_VMEM],
        out_specs=[IN_VMEM] * AHEAD + [IN_HBM] * (len(classes) - AHEAD),
        scratch_shapes=[
            pltpu.VMEM((width, width), F32),
            pltpu.VMEM((2 * width, 2 * width), BF16),
            pltpu.VMEM((width * PITCH, width), F32),
            pltpu.VMEM(blocks.shape, BF16),
            pltpu.VMEM((len(classes) - AHEAD, width * rows, width), BF16),
            pltpu.SemaphoreType.DMA((steps * (1 + len(classes) - AHEAD),)),
        ],
        compiler_params=pltpu.CompilerParams(vmem_limit_bytes=40 * 2**20),
        cost_estimate=pl.CostEstimate(
            flops=flops, bytes_accessed=4 * width**3, transcendentals=0
        ),
        name="contract",
    )(me, in_hbm(blocks), factors)


def receive(block, message, src, out, sums, following):
    rows, ncount, width, _ = src.shape
    blocks = lax.axis_size("sink")
    operands = [block, in_vmem(message), in_vmem(src)]
    specs = [IN_SMEM, IN_VMEM, IN_VMEM]
    shapes = [
        pltpu.HBM((rows, blocks, width, width), BF16),
        pltpu.VMEM((blocks, ncount, width), F32),
    ]
    places = [IN_HBM, IN_VMEM]
    aliases = {}
    if out is not None:
        aliases.update({3: 0, 4: 1})
        operands += [in_hbm(out), in_vmem(sums)]
        specs += places
    if following is not None:
        aliases[len(operands)] = 2
        operands.append(in_hbm(following))
        specs.append(IN_HBM)
        shapes.append(pltpu.HBM(following.shape, following.dtype))
        places = places + [IN_HBM]

    def kernel(*refs):
        block, message, src = refs[:3]
        out, sums = refs[len(operands) : len(operands) + 2]
        wide, stage, sems = refs[-3:]
        if 4 in aliases:
            sums[...] = refs[4][...]
        index = block[0]
        wide[...] = message[...].astype(F32)
        stores = []
        for r in range(rows):
            stage[r] = wide[pl.ds(r, width, stride=rows), :].astype(BF16)
            stores.append(pltpu.make_async_copy(stage.at[r], out.at[r, index], sems.at[r]))
            stores[-1].start()
        for c in range(ncount):
            total = jnp.zeros((8, width), F32)
            for r in range(rows):
                product = stage[r].astype(F32) * src[r, c].astype(F32)
                total = total + jnp.sum(product.reshape(width // 8, 8, width), axis=0)
            sums[index, pl.ds(c, 1)] = jnp.sum(total, axis=0, keepdims=True)
        for store in stores:
            store.wait()

    results = pl.pallas_call(
        kernel,
        out_shape=shapes,
        in_specs=specs,
        out_specs=places,
        scratch_shapes=[
            pltpu.VMEM((rows * width, width), F32),
            pltpu.VMEM((rows, width, width), BF16),
            pltpu.SemaphoreType.DMA((rows,)),
        ],
        input_output_aliases=aliases,
        cost_estimate=pl.CostEstimate(flops=0, bytes_accessed=0, transcendentals=0),
        name="receive",
    )(*operands)
    return results if following is not None else (*results, None)


def determinant(correlation, pairs, tsources):
    ncount = correlation.shape[-1]
    grid = correlation.reshape(tsources, -1, NMOM, ncount)
    momenta = jnp.arange(NMOM, dtype=jnp.int32)
    pick_first = (pairs[:, 0][:, None] == momenta[None, :]).astype(F32)
    pick_second = (pairs[:, 1][:, None] == momenta[None, :]).astype(F32)
    first_one = jnp.einsum("pm,stmc->stpc", pick_first, grid, precision=lax.Precision.HIGHEST)
    second_one = jnp.einsum("pm,stmc->stpc", pick_second, grid, precision=lax.Precision.HIGHEST)
    return first_one[..., 0] * second_one[..., 1] - first_one[..., 1] * second_one[..., 0]


def by_classes(blocks, peram, src_blocks, sink_spin, src_spin, pairs):
    devices = lax.axis_size("sink")
    position = lax.axis_index("sink").astype(jnp.int32)
    picked = pick(peram, sink_spin, src_spin)
    factors = lax.all_to_all(picked, "sink", split_axis=0, concat_axis=0, tiled=True)
    far = list(range(devices // 2, devices))
    near = list(range(devices // 2 - 1, 0, -1))
    far = [d for pair in zip(far[: len(far) // 2], far[len(far) // 2 :]) for d in pair]
    order = []
    for f, c in zip(far, near + [0]):
        order += [f, c]
    order = order[:-2] + order[:-3:-1]
    sent = [d for d in order if d]
    messages = dict(zip(order, contract(position.reshape(1), blocks, factors, order)))

    def send(d, message):
        return lax.ppermute(message, "sink", [(i, i ^ d) for i in range(devices)])

    come = {d: send(d, messages[d]) for d in sent[:AHEAD]}
    come[0] = messages[0]
    out = sums = None
    for step, d in enumerate(order):
        ahead = sent[step + AHEAD] if step + AHEAD < len(sent) else None
        out, sums, following = receive(
            (position ^ d).reshape(1),
            come[d],
            src_blocks,
            out,
            sums,
            None if ahead is None else messages[ahead],
        )
        if ahead is not None:
            come[ahead] = send(ahead, following)
    shift = 1
    while shift < devices:
        sums = sums + send(shift, sums)
        shift *= 2
    correlation = jnp.sum(sums, axis=-1)
    return out, determinant(correlation, pairs, 1)


def by_all_to_all(blocks, peram, src_blocks, sink_spin, src_spin, pairs):
    width = blocks.shape[1]
    tsources = src_spin.shape[0]
    devices = lax.axis_size("sink")
    position = lax.axis_index("sink")
    per_rows = peram.shape[0]
    own_source = (position * per_rows + jnp.arange(per_rows, dtype=jnp.int32)) // width
    target_time = jnp.arange(devices, dtype=jnp.int32) // NMOM
    codes = 4 * sink_spin[None, :, :] + src_spin[own_source][:, None, :]
    picked = peram[
        jnp.arange(per_rows, dtype=jnp.int32)[:, None, None], target_time[None, :, None], codes, :
    ]
    incoming = lax.all_to_all(picked, "sink", split_axis=1, concat_axis=0, tiled=True)
    factors = incoming.reshape(tsources, width, 3, width)

    def transform(source):
        first = dot(blocks.reshape(-1, width), factors[source, :, 2]).astype(BF16)
        second = jnp.einsum(
            "ijk,jJ->iJk",
            first.reshape(blocks.shape),
            factors[source, :, 1],
            preferred_element_type=F32,
        ).astype(BF16)
        return jnp.einsum(
            "iI,iJk->IJk", factors[source, :, 0], second, preferred_element_type=F32
        ).astype(BF16)

    sending = jnp.stack([transform(s) for s in range(tsources)])
    sending = sending.reshape(tsources * width, 1, width, width)
    regrouped = lax.all_to_all(sending, "sink", split_axis=0, concat_axis=1, tiled=True)
    out_rows = regrouped.shape[0]
    row_source = (position * out_rows + jnp.arange(out_rows, dtype=jnp.int32)) // width
    sums = jnp.einsum("rbjk,rcjk->rbc", regrouped, src_blocks, preferred_element_type=F32)
    selector = (row_source[:, None] == jnp.arange(tsources, dtype=jnp.int32)[None, :]).astype(F32)
    local = jnp.einsum("rs,rbc->sbc", selector, sums, precision=lax.Precision.HIGHEST)
    return regrouped, determinant(lax.psum(local, "sink"), pairs, tsources)


def body(blocks, peram, src_blocks, sink_spin, src_spin, pairs):
    devices = lax.axis_size("sink")
    rows = src_blocks.shape[0]
    small = devices in (8, 16, 32) and src_spin.shape[0] == 1 and rows % 8 == 0
    run = by_classes if small else by_all_to_all
    return run(blocks, peram, src_blocks, sink_spin, src_spin, pairs)


def solution(mesh):
    placed = (
        P(("groups", "sink"), None, None),
        P(("groups", "sink"), None, None, None),
        P(("groups", "sink"), None, None, None),
        P(),
        P(),
        P(),
    )
    return jax.shard_map(
        body,
        mesh=mesh,
        in_specs=placed,
        out_specs=(P(("groups", "sink"), None, None, None), P("groups", None, None)),
        check_vma=False,
    )
```

time: 189 us -> 132 us (0.70)
  blocking collectives: 62.2 us -> 0 us
  starting transfers between devices: 4.84 us -> 38.9 us
  local copies, waits for them, and re-layouts: 23.3 us -> 0.02 us
  Pallas kernels: 0 us -> 22.2 us
  matrix products: 17.9 us -> 0.44 us
  waiting for transfers between devices: 77.6 us -> 68.5 us
    all_to_all x1, waiting for transfers between devices: 77.6 us -> 7.4 us  [by_classes(): lax.all_to_all(picked, 'sink', split_axis=0, concat_axis=0, tiled=True)]
    ppermute x0 -> x19, waiting for transfers between devices: none -> 61.1 us  [send(): return lax.ppermute(message, 'sink', [(i, i ^ d) for i in range(devices)])]
    psum x1 -> x0, blocking collectives: 47.6 us -> none  [body(): correlation = lax.psum(local_correlation, 'sink')]
    ppermute x0 -> x19, starting transfers between devices: none -> 31.5 us  [send(): return lax.ppermute(message, 'sink', [(i, i ^ d) for i in range(devices)])]
    pallas_call x0 -> x18, Pallas kernels: none -> 22.2 us  [the longest x16 13 us: receive(): pl.pallas_call(kernel, out_shape=shapes, in_specs=specs, out_specs=places...]
    dot_general x7 -> x2, matrix products: 17.9 us -> 0.44 us  [the longest x1 0.23 us: determinant(): jnp.einsum('pm,stmc->stpc', pick_first, grid, precision=lax.Precision.HIG...]
    all_to_all x1 -> x0, blocking collectives: 14.6 us -> none  [body(): lax.all_to_all(picked, 'sink', split_axis=1, concat_axis=0, tiled=True)]
    gather x3 -> x0, local copies, waits for them, and re-layouts: 7 us -> none  [body(): peram[jnp.arange(per_rows, dtype=jnp.int32)[:, None, None], target_time[N...]
  transfers between devices with their start and end apart: 1 -> 20, of which waited for: 1 -> 11; matrix products, arithmetic and copies ran while one was open for 0% -> 0% of each run, Pallas kernels for 0% -> 9%
where the time goes in v1:
time: 132 us
  waiting for transfers between devices  68.5 us (52%)
  starting transfers between devices  38.9 us (29%)
  Pallas kernels  22.2 us (17%)
    ppermute x19, waiting for transfers between devices, send(): return lax.ppermute(message, 'sink', [(i, i ^ d) for i in range(devices)])  61.1 us
    ppermute x19, starting transfers between devices, send(): return lax.ppermute(message, 'sink', [(i, i ^ d) for i in range(devices)])  31.5 us
    pallas_call x16, Pallas kernels, receive(): pl.pallas_call(kernel, out_shape=shapes, in_specs=specs, out_specs=places...  13 us
    pallas_call x1, Pallas kernels, contract(): pl.pallas_call(kernel, out_shape=[pltpu.VMEM((width * rows, width), BF16)...  7.47 us
    all_to_all x1, waiting for transfers between devices, by_classes(): lax.all_to_all(picked, 'sink', split_axis=0, concat_axis=0, tiled=True)  7.4 us
    all_to_all x1, starting transfers between devices, by_classes(): lax.all_to_all(picked, 'sink', split_axis=0, concat_axis=0, tiled=True)  7.39 us
  transfers between devices with their start and end apart: 20, of which 11 were waited for; matrix products, arithmetic and copies ran while one was open for 0% of the time, Pallas kernels for 9%

profile of v1, /device:TPU:0, one launch (start us, length us, event | category | flops | bytes accessed | tf_op | source)
XLA Modules:
  0.0 131.6 jit_solution(15978827374606346493)
XLA Ops:
  0.6 1.7 %pick.1 = bf16[16,3,8,128]{3,2,1,0:T(8,128)(2,1)} custom-call(s32[3,16]{1,0:T(4,128)} %bitcast.41, s32[1,3]{1,0:T(1,128)} %src_spin.1, bf16[8,4,16,128]{3,2,1,0:T(8,128)(2,1)} %peram.1), custom_call_target="tpu_custom_call" | custom-call | tf_op jit(solution)/shard_map/pick/pallas_call | solution.py:44
  2.3 7.4 %all-to-all-start = ((bf16[16,3,8,128]{3,2,1,0:T(8,128)(2,1)}), bf16[16,3,8,128]{3,2,1,0:T(8,128)(2,1)S(1)}, u32[]{:S(2)}, u32[]{:S(2)}) async-start(bf16[16,3,8,128]{3,2,1,0:T(8,128)(2,1)} %pick.1), calls=%async_computation | async-start | bytes 196608 | tf_op jit(solution)/shard_map/all_to_all | solution.py:222
  9.7 7.4 %all-to-all-done.factors = bf16[16,3,8,128]{3,2,1,0:T(8,128)(2,1)S(1)} async-done(((bf16[16,3,8,128]{3,2,1,0:T(8,128)(2,1)}), bf16[16,3,8,128]{3,2,1,0:T(8,128)(2,1)S(1)}, u32[]{:S(2)}, u32[]{:S(2)}) %all-to-all-start) | async-done | bytes 98336 | tf_op jit(solution)/shard_map/all_to_all | solution.py:222
  17.1 7.5 %contract.1 = (bf16[1024,128]{1,0:T(8,128)(2,1)S(1)}, bf16[1024,128]{1,0:T(8,128)(2,1)S(1)}, bf16[1024,128]{1,0:T(8,128)(2,1)S(1)}, bf16[1024,128]{1,0:T(8,128)(...) custom-call(s32[1]{0:T(128)} %bitcast.3.me.refs_0_, ...), custom_call_target="tpu_custom_call" | custom-call | flops 1610612736 | bytes 8388608 | tf_op jit(solution)/shard_map/contract/pallas_call | solution.py:124
  24.6 0.3 collective-permute-start.4
  24.9 0.6 collective-permute-start.3
  25.5 2.5 %collective-permute-start.2 = (bf16[1024,128]{1,0:T(8,128)(2,1)S(1)}, bf16[1024,128]{1,0:T(8,128)(2,1)S(1)}, u32[]{:S(2)}, u32[]{:S(2)}) collective-permute-start(bf16[1024,128]{1,0:T(8,128)(2,1)S(1)} %get-tuple-element.62), channel_id=1, source_target_pairs={{0,12},{1,13},{2,14},{3,15},{4,8},{5,9},{6,10},{7,11},{8,4},{9,5},... | collective-permute-start | bytes 786440 | tf_op jit(solution)/shard_map/ppermute | solution.py:234
  28.0 0.5 collective-permute-start.1
  28.5 1.8 %collective-permute-start = (bf16[1024,128]{1,0:T(8,128)(2,1)S(1)}, bf16[1024,128]{1,0:T(8,128)(2,1)S(1)}, u32[]{:S(2)}, u32[]{:S(2)}) collective-permute-start(bf16[1024,128]{1,0:T(8,128)(2,1)S(1)} %get-tuple-element.60), channel_id=1, source_target_pairs={{0,9},{1,8},{2,11},{3,10},{4,13},{5,12},{6,15},{7,14},{8,1},{9,0},... | collective-permute-start | bytes 786440 | tf_op jit(solution)/shard_map/ppermute | solution.py:234
  30.3 9.3 %collective-permute-done.4.refs_1_ = bf16[1024,128]{1,0:T(8,128)(2,1)S(1)} collective-permute-done((bf16[1024,128]{1,0:T(8,128)(2,1)S(1)}, bf16[1024,128]{1,0:T(8,128)(2,1)S(1)}, u32[]{:S(2)}, u32[]{:S(2)}) %collective-permute-start.4) | collective-permute-done | bytes 262176 | tf_op jit(solution)/shard_map/ppermute | solution.py:234
  39.7 0.8 receive.16
  40.6 4.8 %collective-permute-done.3.refs_1_ = bf16[1024,128]{1,0:T(8,128)(2,1)S(1)} collective-permute-done((bf16[1024,128]{1,0:T(8,128)(2,1)S(1)}, bf16[1024,128]{1,0:T(8,128)(2,1)S(1)}, u32[]{:S(2)}, u32[]{:S(2)}) %collective-permute-start.3) | collective-permute-done | bytes 262176 | tf_op jit(solution)/shard_map/ppermute | solution.py:234
  45.3 0.8 receive.17
  46.1 1.6 %collective-permute-start.8 = (bf16[1024,128]{1,0:T(8,128)(2,1)}, bf16[1024,128]{1,0:T(8,128)(2,1)S(1)}, u32[]{:S(2)}, u32[]{:S(2)}) collective-permute-start(bf16[1024,128]{1,0:T(8,128)(2,1)} %get-tuple-element.81), channel_id=1, source_target_pairs={{0,13},{1,12},{2,15},{3,14},{4,9},{5,8},{6,11},{7,10},{8,5},{9,4},... | collective-permute-start | bytes 786440 | tf_op jit(solution)/shard_map/ppermute | solution.py:234
  47.8 0.8 receive.18
  48.6 3.8 %collective-permute-start.7 = (bf16[1024,128]{1,0:T(8,128)(2,1)}, bf16[1024,128]{1,0:T(8,128)(2,1)S(1)}, u32[]{:S(2)}, u32[]{:S(2)}) collective-permute-start(bf16[1024,128]{1,0:T(8,128)(2,1)} %get-tuple-element.80), channel_id=1, source_target_pairs={{0,4},{1,5},{2,6},{3,7},{4,0},{5,1},{6,2},{7,3},{8,12},{9,13},{10,... | collective-permute-start | bytes 786440 | tf_op jit(solution)/shard_map/ppermute | solution.py:234
  52.4 0.8 receive.19
  53.2 0.5 collective-permute-start.6
  53.7 7.7 %collective-permute-done.refs_1_ = bf16[1024,128]{1,0:T(8,128)(2,1)S(1)} collective-permute-done((bf16[1024,128]{1,0:T(8,128)(2,1)S(1)}, bf16[1024,128]{1,0:T(8,128)(2,1)S(1)}, u32[]{:S(2)}, u32[]{:S(2)}) %collective-permute-start) | collective-permute-done | bytes 262176 | tf_op jit(solution)/shard_map/ppermute | solution.py:234
  61.4 0.8 receive.20
  62.2 1.4 %collective-permute-start.5 = (bf16[1024,128]{1,0:T(8,128)(2,1)}, bf16[1024,128]{1,0:T(8,128)(2,1)S(1)}, u32[]{:S(2)}, u32[]{:S(2)}) collective-permute-start(bf16[1024,128]{1,0:T(8,128)(2,1)} %get-tuple-element.78), channel_id=1, source_target_pairs={{0,3},{1,2},{2,1},{3,0},{4,7},{5,6},{6,5},{7,4},{8,11},{9,10},{10,... | collective-permute-start | bytes 786440 | tf_op jit(solution)/shard_map/ppermute | solution.py:234
  63.6 0.8 receive.21
  64.4 5.3 %collective-permute-start.14 = (bf16[1024,128]{1,0:T(8,128)(2,1)}, bf16[1024,128]{1,0:T(8,128)(2,1)S(1)}, u32[]{:S(2)}, u32[]{:S(2)}) collective-permute-start(bf16[1024,128]{1,0:T(8,128)(2,1)} %get-tuple-element.103), channel_id=1, source_target_pairs={{0,14},{1,15},{2,12},{3,13},{4,10},{5,11},{6,8},{7,9},{8,6},{9,7},... | collective-permute-start | bytes 786440 | tf_op jit(solution)/shard_map/ppermute | solution.py:234
  69.8 0.8 receive.22
  70.7 1.9 %collective-permute-done.7.refs_1_ = bf16[1024,128]{1,0:T(8,128)(2,1)S(1)} collective-permute-done((bf16[1024,128]{1,0:T(8,128)(2,1)}, bf16[1024,128]{1,0:T(8,128)(2,1)S(1)}, u32[]{:S(2)}, u32[]{:S(2)}) %collective-permute-start.7) | collective-permute-done | bytes 262176 | tf_op jit(solution)/shard_map/ppermute | solution.py:234
  72.6 0.8 receive.23
  73.4 3.4 %collective-permute-start.12 = (bf16[1024,128]{1,0:T(8,128)(2,1)}, bf16[1024,128]{1,0:T(8,128)(2,1)S(1)}, u32[]{:S(2)}, u32[]{:S(2)}) collective-permute-start(bf16[1024,128]{1,0:T(8,128)(2,1)} %get-tuple-element.101), channel_id=1, source_target_pairs={{0,11},{1,10},{2,9},{3,8},{4,15},{5,14},{6,13},{7,12},{8,3},{9,2},... | collective-permute-start | bytes 786440 | tf_op jit(solution)/shard_map/ppermute | solution.py:234
  76.8 18.7 %collective-permute-done.6.refs_1_ = bf16[1024,128]{1,0:T(8,128)(2,1)S(1)} collective-permute-done((bf16[1024,128]{1,0:T(8,128)(2,1)}, bf16[1024,128]{1,0:T(8,128)(2,1)S(1)}, u32[]{:S(2)}, u32[]{:S(2)}) %collective-permute-start.6) | collective-permute-done | bytes 262176 | tf_op jit(solution)/shard_map/ppermute | solution.py:234
  95.5 0.8 receive.24
  96.4 0.8 receive.25
  97.2 2.5 %collective-permute-start.10 = (bf16[1024,128]{1,0:T(8,128)(2,1)}, bf16[1024,128]{1,0:T(8,128)(2,1)S(1)}, u32[]{:S(2)}, u32[]{:S(2)}) collective-permute-start(bf16[1024,128]{1,0:T(8,128)(2,1)} %get-tuple-element.98), channel_id=1, source_target_pairs={{0,15},{1,14},{2,13},{3,12},{4,11},{5,10},{6,9},{7,8},{8,7},{9,6},... | collective-permute-start | bytes 786440 | tf_op jit(solution)/shard_map/ppermute | solution.py:234
  99.7 0.8 receive.26
  100.6 0.8 receive.27
  101.4 10.5 %collective-permute-done.12.refs_1_ = bf16[1024,128]{1,0:T(8,128)(2,1)S(1)} collective-permute-done((bf16[1024,128]{1,0:T(8,128)(2,1)}, bf16[1024,128]{1,0:T(8,128)(2,1)S(1)}, u32[]{:S(2)}, u32[]{:S(2)}) %collective-permute-start.12) | collective-permute-done | bytes 262176 | tf_op jit(solution)/shard_map/ppermute | solution.py:234
  111.9 0.8 receive.28
  112.8 0.8 receive.29
  113.6 0.8 receive.30
  114.4 0.8 receive.31
  115.3 0.3 collective-permute-start.15
  115.6 1.0 collective-permute-done.15
  116.5 1.3 %collective-permute-start.16 = (f32[16,2,128]{2,1,0:T(2,128)S(1)}, f32[16,2,128]{2,1,0:T(2,128)S(1)}, u32[]{:S(2)}, u32[]{:S(2)}) collective-permute-start(f32[16,2,128]{2,1,0:T(2,128)S(1)} %add.12), channel_id=1, source_target_pairs={{0,2},{1,3},{2,0},{3,1},{4,6},{5,7},{6,4},{7,5},{8,10},{9,11},{10,... | collective-permute-start | bytes 49160 | tf_op jit(solution)/shard_map/ppermute | solution.py:234
  117.9 2.5 %collective-permute-done.16 = f32[16,2,128]{2,1,0:T(2,128)S(1)} collective-permute-done((f32[16,2,128]{2,1,0:T(2,128)S(1)}, f32[16,2,128]{2,1,0:T(2,128)S(1)}, u32[]{:S(2)}, u32[]{:S(2)}) %collective-permute-start.16) | collective-permute-done | bytes 16416 | tf_op jit(solution)/shard_map/ppermute | solution.py:234
  120.3 3.7 %collective-permute-start.17 = (f32[16,2,128]{2,1,0:T(2,128)S(1)}, f32[16,2,128]{2,1,0:T(2,128)S(1)}, u32[]{:S(2)}, u32[]{:S(2)}) collective-permute-start(f32[16,2,128]{2,1,0:T(2,128)S(1)} %add.13), channel_id=1, source_target_pairs={{0,4},{1,5},{2,6},{3,7},{4,0},{5,1},{6,2},{7,3},{8,12},{9,13},{10,... | collective-permute-start | bytes 49160 | tf_op jit(solution)/shard_map/ppermute | solution.py:234
  124.1 1.7 %collective-permute-done.17 = f32[16,2,128]{2,1,0:T(2,128)S(1)} collective-permute-done((f32[16,2,128]{2,1,0:T(2,128)S(1)}, f32[16,2,128]{2,1,0:T(2,128)S(1)}, u32[]{:S(2)}, u32[]{:S(2)}) %collective-permute-start.17) | collective-permute-done | bytes 16416 | tf_op jit(solution)/shard_map/ppermute | solution.py:234
  125.8 1.7 %collective-permute-start.18 = (f32[16,2,128]{2,1,0:T(2,128)S(1)}, f32[16,2,128]{2,1,0:T(2,128)S(1)}, u32[]{:S(2)}, u32[]{:S(2)}) collective-permute-start(f32[16,2,128]{2,1,0:T(2,128)S(1)} %add.14), channel_id=1, source_target_pairs={{0,8},{1,9},{2,10},{3,11},{4,12},{5,13},{6,14},{7,15},{8,0},{9,1},... | collective-permute-start | bytes 49160 | tf_op jit(solution)/shard_map/ppermute | solution.py:234
  127.5 3.0 %collective-permute-done.18 = f32[16,2,128]{2,1,0:T(2,128)S(1)} collective-permute-done((f32[16,2,128]{2,1,0:T(2,128)S(1)}, f32[16,2,128]{2,1,0:T(2,128)S(1)}, u32[]{:S(2)}, u32[]{:S(2)}) %collective-permute-start.18) | collective-permute-done | bytes 16416 | tf_op jit(solution)/shard_map/ppermute | solution.py:234
  130.8 0.2 convolution_bitcast_fusion.1
  131.0 0.6 fusion
  (24 shorter events, 0.6 us)
Async XLA Ops:
  0.6 39.0 %copy-start = (bf16[8,2,128,128]{3,2,1,0:T(8,128)(2,1)S(1)}, bf16[8,2,128,128]{3,2,1,0:T(8,128)(2,1)}, u32[]{:S(2)}) copy-start(bf16[8,2,128,128]{3,2,1,0:T(8,128)(2,1)} %refs_2_.31) | copy-start | bytes 1572868
  2.3 14.8 %all-to-all-start = ((bf16[16,3,8,128]{3,2,1,0:T(8,128)(2,1)}), bf16[16,3,8,128]{3,2,1,0:T(8,128)(2,1)S(1)}, u32[]{:S(2)}, u32[]{:S(2)}) async-start(bf16[16,3,8,128]{3,2,1,0:T(8,128)(2,1)} %pick.1), calls=%async_computation | async-start | bytes 196608 | tf_op jit(solution)/shard_map/all_to_all | solution.py:222
  24.6 15.0 %collective-permute-start.4 = (bf16[1024,128]{1,0:T(8,128)(2,1)S(1)}, bf16[1024,128]{1,0:T(8,128)(2,1)S(1)}, u32[]{:S(2)}, u32[]{:S(2)}) collective-permute-start(bf16[1024,128]{1,0:T(8,128)(2,1)S(1)} %get-tuple-element.64), channel_id=1, source_target_pairs={{0,8},{1,9},{2,10},{3,11},{4,12},{5,13},{6,14},{7,15},{8,0},{9,1},... | collective-permute-start | bytes 786440 | tf_op jit(solution)/shard_map/ppermute | solution.py:234
  24.9 20.4 %collective-permute-start.3 = (bf16[1024,128]{1,0:T(8,128)(2,1)S(1)}, bf16[1024,128]{1,0:T(8,128)(2,1)S(1)}, u32[]{:S(2)}, u32[]{:S(2)}) collective-permute-start(bf16[1024,128]{1,0:T(8,128)(2,1)S(1)} %get-tuple-element.63), channel_id=1, source_target_pairs={{0,7},{1,6},{2,5},{3,4},{4,3},{5,2},{6,1},{7,0},{8,15},{9,14},{10,... | collective-permute-start | bytes 786440 | tf_op jit(solution)/shard_map/ppermute | solution.py:234
  25.5 22.3 %collective-permute-start.2 = (bf16[1024,128]{1,0:T(8,128)(2,1)S(1)}, bf16[1024,128]{1,0:T(8,128)(2,1)S(1)}, u32[]{:S(2)}, u32[]{:S(2)}) collective-permute-start(bf16[1024,128]{1,0:T(8,128)(2,1)S(1)} %get-tuple-element.62), channel_id=1, source_target_pairs={{0,12},{1,13},{2,14},{3,15},{4,8},{5,9},{6,10},{7,11},{8,4},{9,5},... | collective-permute-start | bytes 786440 | tf_op jit(solution)/shard_map/ppermute | solution.py:234
  28.0 24.4 %collective-permute-start.1 = (bf16[1024,128]{1,0:T(8,128)(2,1)S(1)}, bf16[1024,128]{1,0:T(8,128)(2,1)S(1)}, u32[]{:S(2)}, u32[]{:S(2)}) collective-permute-start(bf16[1024,128]{1,0:T(8,128)(2,1)S(1)} %get-tuple-element.61), channel_id=1, source_target_pairs={{0,6},{1,7},{2,4},{3,5},{4,2},{5,3},{6,0},{7,1},{8,14},{9,15},{10,... | collective-permute-start | bytes 786440 | tf_op jit(solution)/shard_map/ppermute | solution.py:234
  28.5 32.8 %collective-permute-start = (bf16[1024,128]{1,0:T(8,128)(2,1)S(1)}, bf16[1024,128]{1,0:T(8,128)(2,1)S(1)}, u32[]{:S(2)}, u32[]{:S(2)}) collective-permute-start(bf16[1024,128]{1,0:T(8,128)(2,1)S(1)} %get-tuple-element.60), channel_id=1, source_target_pairs={{0,9},{1,8},{2,11},{3,10},{4,13},{5,12},{6,15},{7,14},{8,1},{9,0},... | collective-permute-start | bytes 786440 | tf_op jit(solution)/shard_map/ppermute | solution.py:234
  40.5 23.1 %collective-permute-start.9 = (bf16[1024,128]{1,0:T(8,128)(2,1)}, bf16[1024,128]{1,0:T(8,128)(2,1)S(1)}, u32[]{:S(2)}, u32[]{:S(2)}) collective-permute-start(bf16[1024,128]{1,0:T(8,128)(2,1)} %get-tuple-element.82), channel_id=1, source_target_pairs={{0,5},{1,4},{2,7},{3,6},{4,1},{5,0},{6,3},{7,2},{8,13},{9,12},{10,... | collective-permute-start | bytes 786440 | tf_op jit(solution)/shard_map/ppermute | solution.py:234
  46.1 23.6 %collective-permute-start.8 = (bf16[1024,128]{1,0:T(8,128)(2,1)}, bf16[1024,128]{1,0:T(8,128)(2,1)S(1)}, u32[]{:S(2)}, u32[]{:S(2)}) collective-permute-start(bf16[1024,128]{1,0:T(8,128)(2,1)} %get-tuple-element.81), channel_id=1, source_target_pairs={{0,13},{1,12},{2,15},{3,14},{4,9},{5,8},{6,11},{7,10},{8,5},{9,4},... | collective-permute-start | bytes 786440 | tf_op jit(solution)/shard_map/ppermute | solution.py:234
  48.6 24.0 %collective-permute-start.7 = (bf16[1024,128]{1,0:T(8,128)(2,1)}, bf16[1024,128]{1,0:T(8,128)(2,1)S(1)}, u32[]{:S(2)}, u32[]{:S(2)}) collective-permute-start(bf16[1024,128]{1,0:T(8,128)(2,1)} %get-tuple-element.80), channel_id=1, source_target_pairs={{0,4},{1,5},{2,6},{3,7},{4,0},{5,1},{6,2},{7,3},{8,12},{9,13},{10,... | collective-permute-start | bytes 786440 | tf_op jit(solution)/shard_map/ppermute | solution.py:234
  53.2 42.3 %collective-permute-start.6 = (bf16[1024,128]{1,0:T(8,128)(2,1)}, bf16[1024,128]{1,0:T(8,128)(2,1)S(1)}, u32[]{:S(2)}, u32[]{:S(2)}) collective-permute-start(bf16[1024,128]{1,0:T(8,128)(2,1)} %get-tuple-element.79), channel_id=1, source_target_pairs={{0,10},{1,11},{2,8},{3,9},{4,14},{5,15},{6,12},{7,13},{8,2},{9,3},... | collective-permute-start | bytes 786440 | tf_op jit(solution)/shard_map/ppermute | solution.py:234
  62.2 34.2 %collective-permute-start.5 = (bf16[1024,128]{1,0:T(8,128)(2,1)}, bf16[1024,128]{1,0:T(8,128)(2,1)S(1)}, u32[]{:S(2)}, u32[]{:S(2)}) collective-permute-start(bf16[1024,128]{1,0:T(8,128)(2,1)} %get-tuple-element.78), channel_id=1, source_target_pairs={{0,3},{1,2},{2,1},{3,0},{4,7},{5,6},{6,5},{7,4},{8,11},{9,10},{10,... | collective-permute-start | bytes 786440 | tf_op jit(solution)/shard_map/ppermute | solution.py:234
  64.4 35.3 %collective-permute-start.14 = (bf16[1024,128]{1,0:T(8,128)(2,1)}, bf16[1024,128]{1,0:T(8,128)(2,1)S(1)}, u32[]{:S(2)}, u32[]{:S(2)}) collective-permute-start(bf16[1024,128]{1,0:T(8,128)(2,1)} %get-tuple-element.103), channel_id=1, source_target_pairs={{0,14},{1,15},{2,12},{3,13},{4,10},{5,11},{6,8},{7,9},{8,6},{9,7},... | collective-permute-start | bytes 786440 | tf_op jit(solution)/shard_map/ppermute | solution.py:234
  70.6 30.0 %collective-permute-start.13 = (bf16[1024,128]{1,0:T(8,128)(2,1)}, bf16[1024,128]{1,0:T(8,128)(2,1)S(1)}, u32[]{:S(2)}, u32[]{:S(2)}) collective-permute-start(bf16[1024,128]{1,0:T(8,128)(2,1)} %get-tuple-element.102), channel_id=1, source_target_pairs={{0,2},{1,3},{2,0},{3,1},{4,6},{5,7},{6,4},{7,5},{8,10},{9,11},{10,... | collective-permute-start | bytes 786440 | tf_op jit(solution)/shard_map/ppermute | solution.py:234
  73.4 38.5 %collective-permute-start.12 = (bf16[1024,128]{1,0:T(8,128)(2,1)}, bf16[1024,128]{1,0:T(8,128)(2,1)S(1)}, u32[]{:S(2)}, u32[]{:S(2)}) collective-permute-start(bf16[1024,128]{1,0:T(8,128)(2,1)} %get-tuple-element.101), channel_id=1, source_target_pairs={{0,11},{1,10},{2,9},{3,8},{4,15},{5,14},{6,13},{7,12},{8,3},{9,2},... | collective-permute-start | bytes 786440 | tf_op jit(solution)/shard_map/ppermute | solution.py:234
  96.3 16.5 %collective-permute-start.11 = (bf16[1024,128]{1,0:T(8,128)(2,1)}, bf16[1024,128]{1,0:T(8,128)(2,1)S(1)}, u32[]{:S(2)}, u32[]{:S(2)}) collective-permute-start(bf16[1024,128]{1,0:T(8,128)(2,1)} %get-tuple-element.100), channel_id=1, source_target_pairs={{0,1},{1,0},{2,3},{3,2},{4,5},{5,4},{6,7},{7,6},{8,9},{9,8},{10,11... | collective-permute-start | bytes 786440 | tf_op jit(solution)/shard_map/ppermute | solution.py:234
  97.2 17.2 %collective-permute-start.10 = (bf16[1024,128]{1,0:T(8,128)(2,1)}, bf16[1024,128]{1,0:T(8,128)(2,1)S(1)}, u32[]{:S(2)}, u32[]{:S(2)}) collective-permute-start(bf16[1024,128]{1,0:T(8,128)(2,1)} %get-tuple-element.98), channel_id=1, source_target_pairs={{0,15},{1,14},{2,13},{3,12},{4,11},{5,10},{6,9},{7,8},{8,7},{9,6},... | collective-permute-start | bytes 786440 | tf_op jit(solution)/shard_map/ppermute | solution.py:234
  111.9 1.7 %copy-start.1 = (bf16[1024,128]{1,0:T(8,128)(2,1)S(1)}, bf16[1024,128]{1,0:T(8,128)(2,1)}, u32[]{:S(2)}) copy-start(bf16[1024,128]{1,0:T(8,128)(2,1)} %get-tuple-element.99.refs_1_) | copy-start | bytes 786436
  113.6 13.9 %copy-start.2 = (s32[4,2]{0,1:T(2,128)S(1)}, s32[4,2]{0,1:T(2,128)}, u32[]{:S(2)}) copy-start(s32[4,2]{0,1:T(2,128)} %param.11) | copy-start | bytes 100
  115.3 1.2 collective-permute-start.15
  116.5 3.8 %collective-permute-start.16 = (f32[16,2,128]{2,1,0:T(2,128)S(1)}, f32[16,2,128]{2,1,0:T(2,128)S(1)}, u32[]{:S(2)}, u32[]{:S(2)}) collective-permute-start(f32[16,2,128]{2,1,0:T(2,128)S(1)} %add.12), channel_id=1, source_target_pairs={{0,2},{1,3},{2,0},{3,1},{4,6},{5,7},{6,4},{7,5},{8,10},{9,11},{10,... | collective-permute-start | bytes 49160 | tf_op jit(solution)/shard_map/ppermute | solution.py:234
  120.3 5.4 %collective-permute-start.17 = (f32[16,2,128]{2,1,0:T(2,128)S(1)}, f32[16,2,128]{2,1,0:T(2,128)S(1)}, u32[]{:S(2)}, u32[]{:S(2)}) collective-permute-start(f32[16,2,128]{2,1,0:T(2,128)S(1)} %add.13), channel_id=1, source_target_pairs={{0,4},{1,5},{2,6},{3,7},{4,0},{5,1},{6,2},{7,3},{8,12},{9,13},{10,... | collective-permute-start | bytes 49160 | tf_op jit(solution)/shard_map/ppermute | solution.py:234
  125.8 4.7 %collective-permute-start.18 = (f32[16,2,128]{2,1,0:T(2,128)S(1)}, f32[16,2,128]{2,1,0:T(2,128)S(1)}, u32[]{:S(2)}, u32[]{:S(2)}) collective-permute-start(f32[16,2,128]{2,1,0:T(2,128)S(1)} %add.14), channel_id=1, source_target_pairs={{0,8},{1,9},{2,10},{3,11},{4,12},{5,13},{6,14},{7,15},{8,0},{9,1},... | collective-permute-start | bytes 49160 | tf_op jit(solution)/shard_map/ppermute | solution.py:234

commit v2 on v1

--- a/solution.py
+++ b/solution.py
@@ -14,6 +14,7 @@
 IN_SMEM = pl.BlockSpec(memory_space=pltpu.SMEM)
 IN_HBM = pl.BlockSpec(memory_space=pltpu.HBM)
 AHEAD = 5
+DEPTH = 4
 
 
 def in_hbm(array):
@@ -43,7 +44,7 @@
     blocks = sink_spin.shape[0]
     return pl.pallas_call(
         pick_kernel,
-        out_shape=jax.ShapeDtypeStruct((blocks, 3, rows, width), BF16),
+        out_shape=pltpu.VMEM((blocks, 3, rows, width), BF16),
         in_specs=[IN_SMEM, IN_SMEM, IN_VMEM],
         out_specs=IN_VMEM,
         scratch_shapes=[pltpu.VMEM((times * codes, rows, width), F32)],
@@ -51,20 +52,38 @@
     )(sink_spin.T, src_spin, peram)
 
 
-def contract(me, blocks, factors, classes):
+def left_rows(me, left0, classes, rows):
+    parts = [left0[pl.ds(pl.multiple_of((me ^ d) * rows, rows), rows), :] for d in classes]
+    return jnp.concatenate(parts, 0).astype(BF16)
+
+
+def put_tiles(outs, done, base, rows, width):
+    for index, out in enumerate(outs):
+        tiles = []
+        for product in done:
+            own = product[index * rows : (index + 1) * rows]
+            tiles += [own[:, :width], own[:, width:]]
+        out[pl.ds(base * rows, len(tiles) * rows), :] = jnp.concatenate(tiles, 0).astype(BF16)
+
+
+def contract(blocks, factors, classes, place):
     width = blocks.shape[0]
     rows = factors.shape[2]
-    half = width // 2
-    steps = half // GROUP
-
-    def kernel(me, blocks, factors, *refs):
-        outs, (left0, wide2, second, held, kept, sems) = refs[: len(classes)], refs[len(classes) :]
-        made = [kept.at[q - AHEAD] if q >= AHEAD else out for q, out in enumerate(outs)]
-        copies = []
+    steps = width // 2 // GROUP
+    count = len(classes)
+    shape = (width * rows, width)
+    stored = place is not pltpu.VMEM
+
+    def kernel(blocks, factors, *refs):
+        me = lax.axis_index("sink")
+        outs, (held, left0, wide2, second, sems) = refs[:count], refs[count : count + 5]
+        made = refs[count + 5 :] if stored else outs
+        loads, stores = [], []
         for step in range(steps):
             part = pl.ds(step * 2 * GROUP, 2 * GROUP)
-            copies.append(pltpu.make_async_copy(blocks.at[part], held.at[part], sems.at[step]))
-            copies[-1].start()
+            loads.append(pltpu.make_async_copy(blocks.at[part], held.at[part], sems.at[step]))
+        for step in range(DEPTH):
+            loads[step].start()
         parts = [factors[:, m].astype(F32).reshape(width, width) for m in range(3)]
         left1 = parts[1].T.astype(BF16)
         left0[...] = parts[0].T
@@ -73,9 +92,10 @@
         wide2[...] = jnp.concatenate(
             [jnp.concatenate([right2, zero], 1), jnp.concatenate([zero, right2], 1)], 0
         )
-
         for step in range(steps):
-            copies[step].wait()
+            loads[step].wait()
+            if step + DEPTH < steps:
+                loads[step + DEPTH].start()
             base = step * 2 * GROUP
             pairs = [
                 jnp.concatenate([held[base + 2 * q], held[base + 2 * q + 1]], 1)
@@ -87,67 +107,51 @@
                 for h in range(2):
                     start = (base + 2 * q + h) * PITCH
                     second[pl.ds(start, width), :] = done[:, h * width : (h + 1) * width]
-        left = jnp.concatenate(
-            [left0[pl.ds(pl.multiple_of((me[0] ^ d) * rows, rows), rows), :] for d in classes], 0
-        ).astype(BF16)
-
+        left = left_rows(me, left0, classes, rows)
         for step in range(steps):
             base = step * 2 * GROUP
             done = []
             for q in range(GROUP):
-                right = jnp.concatenate(
-                    [
-                        second[pl.ds(base + 2 * q + h, width, stride=PITCH), :].astype(BF16)
-                        for h in range(2)
-                    ],
-                    1,
+                halves = [
+                    second[pl.ds(base + 2 * q + h, width, stride=PITCH), :].astype(BF16)
+                    for h in range(2)
+                ]
+                done.append(dot(left, jnp.concatenate(halves, 1)))
+            put_tiles(made, done, base, rows, width)
+            part = pl.ds(base * rows, 2 * GROUP * rows)
+            for index in range(count if stored else 0):
+                sem = sems.at[steps + step * count + index]
+                stores.append(
+                    pltpu.make_async_copy(made[index].at[part], outs[index].at[part], sem)
                 )
-                done.append(dot(left, right))
-            for index in range(len(classes)):
-                tiles = []
-                for q in range(GROUP):
-                    own = done[q][index * rows : (index + 1) * rows]
-                    tiles += [own[:, :width], own[:, width:]]
-                part = pl.ds(base * rows, 2 * GROUP * rows)
-                made[index][part, :] = jnp.concatenate(tiles, 0).astype(BF16)
-            for index in range(AHEAD, len(classes)):
-                copies.append(
-                    pltpu.make_async_copy(
-                        made[index].at[part], outs[index].at[part], sems.at[len(copies)]
-                    )
-                )
-                copies[-1].start()
-        for copy in copies[steps:]:
-            copy.wait()
-
-    flops = 2 * 3 * width**4
+                stores[-1].start()
+        for store in stores:
+            store.wait()
+
     return pl.pallas_call(
         kernel,
-        out_shape=[pltpu.VMEM((width * rows, width), BF16)] * AHEAD
-        + [pltpu.HBM((width * rows, width), BF16)] * (len(classes) - AHEAD),
-        in_specs=[IN_SMEM, IN_HBM, IN_VMEM],
-        out_specs=[IN_VMEM] * AHEAD + [IN_HBM] * (len(classes) - AHEAD),
+        out_shape=[place(shape, BF16)] * count,
+        in_specs=[IN_HBM, IN_VMEM],
+        out_specs=[IN_HBM if stored else IN_VMEM] * count,
         scratch_shapes=[
+            pltpu.VMEM(blocks.shape, BF16),
             pltpu.VMEM((width, width), F32),
             pltpu.VMEM((2 * width, 2 * width), BF16),
             pltpu.VMEM((width * PITCH, width), F32),
-            pltpu.VMEM(blocks.shape, BF16),
-            pltpu.VMEM((len(classes) - AHEAD, width * rows, width), BF16),
-            pltpu.SemaphoreType.DMA((steps * (1 + len(classes) - AHEAD),)),
-        ],
+            pltpu.SemaphoreType.DMA((steps * (1 + count) + 1,)),
+        ]
+        + [pltpu.VMEM(shape, BF16)] * (count if stored else 0),
         compiler_params=pltpu.CompilerParams(vmem_limit_bytes=40 * 2**20),
-        cost_estimate=pl.CostEstimate(
-            flops=flops, bytes_accessed=4 * width**3, transcendentals=0
-        ),
+        cost_estimate=pl.CostEstimate(flops=0, bytes_accessed=0, transcendentals=0),
         name="contract",
-    )(me, in_hbm(blocks), factors)
-
-
-def receive(block, message, src, out, sums, following):
+    )(in_hbm(blocks), in_vmem(factors))
+
+
+def receive(d, message, src, out, sums, following):
     rows, ncount, width, _ = src.shape
     blocks = lax.axis_size("sink")
-    operands = [block, in_vmem(message), in_vmem(src)]
-    specs = [IN_SMEM, IN_VMEM, IN_VMEM]
+    operands = [in_vmem(message), in_vmem(src)]
+    specs = [IN_VMEM, IN_VMEM]
     shapes = [
         pltpu.HBM((rows, blocks, width, width), BF16),
         pltpu.VMEM((blocks, ncount, width), F32),
@@ -155,7 +159,7 @@
     places = [IN_HBM, IN_VMEM]
     aliases = {}
     if out is not None:
-        aliases.update({3: 0, 4: 1})
+        aliases.update({2: 0, 3: 1})
         operands += [in_hbm(out), in_vmem(sums)]
         specs += places
     if following is not None:
@@ -166,12 +170,12 @@
         places = places + [IN_HBM]
 
     def kernel(*refs):
-        block, message, src = refs[:3]
+        message, src = refs[:2]
         out, sums = refs[len(operands) : len(operands) + 2]
         wide, stage, sems = refs[-3:]
-        if 4 in aliases:
-            sums[...] = refs[4][...]
-        index = block[0]
+        if 3 in aliases:
+            sums[...] = refs[3][...]
+        index = lax.axis_index("sink") ^ d
         wide[...] = message[...].astype(F32)
         stores = []
         for r in range(rows):
@@ -215,31 +219,61 @@
     return first_one[..., 0] * second_one[..., 1] - first_one[..., 1] * second_one[..., 0]
 
 
+def finish(sums, pairs):
+    devices, _, width = sums.shape
+    times = devices // NMOM
+
+    def kernel(pairs, sums, out):
+        row = jnp.sum(sums[...], axis=0)
+        time = lax.broadcasted_iota(jnp.int32, (times, width), 0)
+        lane = lax.broadcasted_iota(jnp.int32, (times, width), 1)
+        columns = []
+        for p in range(pairs.shape[1]):
+            values = [
+                jnp.sum(
+                    jnp.where(lane == 2 * (NMOM * time + pairs[k, p]) + c, row, 0.0),
+                    axis=1,
+                    keepdims=True,
+                )
+                for k in range(2)
+                for c in range(2)
+            ]
+            columns.append(values[0] * values[3] - values[1] * values[2])
+        out[0] = jnp.concatenate(columns, 1)
+
+    return pl.pallas_call(
+        kernel,
+        out_shape=jax.ShapeDtypeStruct((1, times, pairs.shape[0]), F32),
+        in_specs=[IN_SMEM, IN_VMEM],
+        out_specs=IN_VMEM,
+        name="finish",
+    )(pairs.T, sums)
+
+
 def by_classes(blocks, peram, src_blocks, sink_spin, src_spin, pairs):
     devices = lax.axis_size("sink")
-    position = lax.axis_index("sink").astype(jnp.int32)
+    rows, ncount, width, _ = src_blocks.shape
+
+    def send(d, message):
+        return lax.ppermute(message, "sink", [(i, i ^ d) for i in range(devices)])
+
     picked = pick(peram, sink_spin, src_spin)
     factors = lax.all_to_all(picked, "sink", split_axis=0, concat_axis=0, tiled=True)
     far = list(range(devices // 2, devices))
     near = list(range(devices // 2 - 1, 0, -1))
     far = [d for pair in zip(far[: len(far) // 2], far[len(far) // 2 :]) for d in pair]
-    order = []
-    for f, c in zip(far, near + [0]):
-        order += [f, c]
-    order = order[:-2] + order[:-3:-1]
-    sent = [d for d in order if d]
-    messages = dict(zip(order, contract(position.reshape(1), blocks, factors, order)))
-
-    def send(d, message):
-        return lax.ppermute(message, "sink", [(i, i ^ d) for i in range(devices)])
-
-    come = {d: send(d, messages[d]) for d in sent[:AHEAD]}
-    come[0] = messages[0]
-    out = sums = None
-    for step, d in enumerate(order):
+    sent = []
+    for f, c in zip(far, near + [None]):
+        sent += [f] if c is None else [f, c]
+    early = contract(blocks, factors, sent[:AHEAD], pltpu.VMEM)
+    come = {d: send(d, message) for d, message in zip(sent, early)}
+    rest = sent[AHEAD:] + [0]
+    messages = dict(zip(rest, contract(blocks, factors, rest, pltpu.HBM)))
+    out, sums, _ = receive(0, messages[0], src_blocks, None, None, None)
+    for step, d in enumerate(sent):
         ahead = sent[step + AHEAD] if step + AHEAD < len(sent) else None
         out, sums, following = receive(
-            (position ^ d).reshape(1),
+            d,
             come[d],
             src_blocks,
             out,
@@ -248,12 +282,12 @@
         )
         if ahead is not None:
             come[ahead] = send(ahead, following)
-    shift = 1
-    while shift < devices:
-        sums = sums + send(shift, sums)
-        shift *= 2
-    correlation = jnp.sum(sums, axis=-1)
-    return out, determinant(correlation, pairs, 1)
+    row = jnp.sum(sums, axis=-1).reshape(1, 1, devices * ncount)
+    row = jnp.pad(row, ((0, 0), (0, 0), (0, width - devices * ncount)))
+    rows_of_all = lax.all_to_all(
+        jnp.broadcast_to(row, (devices, 1, width)), "sink", split_axis=0, concat_axis=0, tiled=True
+    )
+    return out, finish(rows_of_all, pairs)
 
 
 def by_all_to_all(blocks, peram, src_blocks, sink_spin, src_spin, pairs):
@@ -296,8 +330,7 @@
 
 def body(blocks, peram, src_blocks, sink_spin, src_spin, pairs):
     devices = lax.axis_size("sink")
-    rows = src_blocks.shape[0]
-    small = devices in (8, 16, 32) and src_spin.shape[0] == 1 and rows % 8 == 0
+    small = devices == 16 and src_spin.shape[0] == 1 and src_blocks.shape[:2] == (8, 2)
     run = by_classes if small else by_all_to_all
     return run(blocks, peram, src_blocks, sink_spin, src_spin, pairs)
 

time: 132 us -> 127 us (0.962)
  blocking collectives: 0 us -> 32.7 us
  waiting for transfers between devices: 68.5 us -> 40.5 us
  starting transfers between devices: 38.9 us -> 22.4 us
  Pallas kernels: 22.2 us -> 29.5 us
    all_to_all x0 -> x2, blocking collectives: none -> 32.7 us  [the longest x1 18.1 us: by_classes(): lax.all_to_all(jnp.broadcast_to(row, (devices, 1, width)), 'sink', split_...]
    ppermute x19 -> x15, waiting for transfers between devices: 61.1 us -> 40.5 us  [send(): return lax.ppermute(message, 'sink', [(i, i ^ d) for i in range(devices)])]
    ppermute x19 -> x15, starting transfers between devices: 31.5 us -> 22.4 us  [send(): return lax.ppermute(message, 'sink', [(i, i ^ d) for i in range(devices)])]
    all_to_all x1 -> x0, waiting for transfers between devices: 7.4 us -> none  [by_classes(): lax.all_to_all(picked, 'sink', split_axis=0, concat_axis=0, tiled=True)]
    all_to_all x1 -> x0, starting transfers between devices: 7.39 us -> none  [by_classes(): lax.all_to_all(picked, 'sink', split_axis=0, concat_axis=0, tiled=True)]
    pallas_call x2 -> x4, Pallas kernels: 9.17 us -> 16.5 us  [the longest x2 14.1 us: contract(): pl.pallas_call(kernel, out_shape=[place(shape, BF16)] * count, in_specs=[...]
  transfers between devices with their start and end apart: 20 -> 15, of which waited for: 11 -> 7; matrix products, arithmetic and copies ran while one was open for 0% -> 0% of each run, Pallas kernels for 9% -> 16%
where the time goes in v2:
time: 127 us
  waiting for transfers between devices  40.5 us (32%)
  blocking collectives  32.7 us (26%)
  Pallas kernels  29.5 us (23%)
  starting transfers between devices  22.4 us (18%)
    ppermute x15, waiting for transfers between devices, send(): return lax.ppermute(message, 'sink', [(i, i ^ d) for i in range(devices)])  40.5 us
    ppermute x15, starting transfers between devices, send(): return lax.ppermute(message, 'sink', [(i, i ^ d) for i in range(devices)])  22.4 us
    all_to_all x1, blocking collectives, by_classes(): lax.all_to_all(jnp.broadcast_to(row, (devices, 1, width)), 'sink', split_...  18.1 us
    all_to_all x1, blocking collectives, by_classes(): lax.all_to_all(picked, 'sink', split_axis=0, concat_axis=0, tiled=True)  14.6 us
    pallas_call x2, Pallas kernels, contract(): pl.pallas_call(kernel, out_shape=[place(shape, BF16)] * count, in_specs=[...  14.1 us
    pallas_call x16, Pallas kernels, receive(): pl.pallas_call(kernel, out_shape=shapes, in_specs=specs, out_specs=places...  13 us
  transfers between devices with their start and end apart: 15, of which 7 were waited for; matrix products, arithmetic and copies ran while one was open for 0% of the time, Pallas kernels for 16%

profile of v2, /device:TPU:0, one launch (start us, length us, event | category | flops | bytes accessed | tf_op | source)
XLA Modules:
  0.0 127.1 jit_solution(11592987697727146332)
XLA Ops:
  0.6 1.0 pick.1
  1.6 14.6 %all_to_all.10.factors = bf16[16,3,8,128]{3,2,1,0:T(8,128)(2,1)S(1)} all-to-all(bf16[16,3,8,128]{3,2,1,0:T(8,128)(2,1)S(1)} %pick.1), channel_id=1, replica_groups=mesh['groups'=2,'sink'=16] {'sink'}, dimensions={0} | all-to-all | bytes 196608 | tf_op jit(solution)/shard_map/all_to_all | solution.py:261
  16.2 6.5 %contract.2 = (bf16[1024,128]{1,0:T(8,128)(2,1)S(1)}, bf16[1024,128]{1,0:T(8,128)(2,1)S(1)}, bf16[1024,128]{1,0:T(8,128)(2,1)S(1)}, bf16[1024,128]{1,0:T(8,128)(2,1)S(1)}, bf16[1024,128]{1,0:T(8,128)(2,1)S(1)}) custom-call(bf16[128,128,128]{2,1,0:T(8,128)(2,1)} %blocks.3, bf16[16,3,8,128]{3,2,1,0:T(8,128)(2,1)S(1)} %all_to_all.10.factors), custom_call_target="tpu_custom_call" | custom-call | tf_op jit(solution)/shard_map/contract/pallas_call | solution.py:131
  22.7 0.2 collective-permute-start.4
  23.0 0.6 collective-permute-start.3
  23.6 2.5 %collective-permute-start.2 = (bf16[1024,128]{1,0:T(8,128)(2,1)S(1)}, bf16[1024,128]{1,0:T(8,128)(2,1)S(1)}, u32[]{:S(2)}, u32[]{:S(2)}) collective-permute-start(bf16[1024,128]{1,0:T(8,128)(2,1)S(1)} %get-tuple-element.62), channel_id=1, source_target_pairs={{0,12},{1,13},{2,14},{3,15},{4,8},{5,9},{6,10},{7,11},{8,4},{9,5},... | collective-permute-start | bytes 786440 | tf_op jit(solution)/shard_map/ppermute | solution.py:258
  26.1 0.5 collective-permute-start.1
  26.6 1.8 %collective-permute-start = (bf16[1024,128]{1,0:T(8,128)(2,1)S(1)}, bf16[1024,128]{1,0:T(8,128)(2,1)S(1)}, u32[]{:S(2)}, u32[]{:S(2)}) collective-permute-start(bf16[1024,128]{1,0:T(8,128)(2,1)S(1)} %get-tuple-element.60), channel_id=1, source_target_pairs={{0,9},{1,8},{2,11},{3,10},{4,13},{5,12},{6,15},{7,14},{8,1},{9,0},... | collective-permute-start | bytes 786440 | tf_op jit(solution)/shard_map/ppermute | solution.py:258
  28.5 7.6 %contract.3 = (bf16[1024,128]{1,0:T(8,128)(2,1)}, bf16[1024,128]{1,0:T(8,128)(2,1)}, bf16[1024,128]{1,0:T(8,128)(2,1)}, bf16[1024,128]{1,0:T(8,128)(2,1)}, bf16[...) custom-call(bf16[128,128,128]{2,1,0:T(8,128)(2,1)} %blocks.3, ...), custom_call_target="tpu_custom_call" | custom-call | tf_op jit(solution)/shard_map/contract/pallas_call | solution.py:131
  36.0 0.9 copy-done.1
  37.0 0.8 receive.16
  37.8 0.0 collective-permute-done.4.refs_0_
  37.8 0.8 receive.17
  38.6 0.9 collective-permute-start.9
  39.5 3.9 %collective-permute-done.3.refs_0_ = bf16[1024,128]{1,0:T(8,128)(2,1)S(1)} collective-permute-done((bf16[1024,128]{1,0:T(8,128)(2,1)S(1)}, bf16[1024,128]{1,0:T(8,128)(2,1)S(1)}, u32[]{:S(2)}, u32[]{:S(2)}) %collective-permute-start.3) | collective-permute-done | bytes 262176 | tf_op jit(solution)/shard_map/ppermute | solution.py:258
  43.4 0.8 receive.18
  44.2 1.6 %collective-permute-start.8 = (bf16[1024,128]{1,0:T(8,128)(2,1)}, bf16[1024,128]{1,0:T(8,128)(2,1)S(1)}, u32[]{:S(2)}, u32[]{:S(2)}) collective-permute-start(bf16[1024,128]{1,0:T(8,128)(2,1)} %get-tuple-element.84), channel_id=1, source_target_pairs={{0,13},{1,12},{2,15},{3,14},{4,9},{5,8},{6,11},{7,10},{8,5},{9,4},... | collective-permute-start | bytes 786440 | tf_op jit(solution)/shard_map/ppermute | solution.py:258
  45.9 0.8 receive.19
  46.7 3.8 %collective-permute-start.7 = (bf16[1024,128]{1,0:T(8,128)(2,1)}, bf16[1024,128]{1,0:T(8,128)(2,1)S(1)}, u32[]{:S(2)}, u32[]{:S(2)}) collective-permute-start(bf16[1024,128]{1,0:T(8,128)(2,1)} %get-tuple-element.83), channel_id=1, source_target_pairs={{0,4},{1,5},{2,6},{3,7},{4,0},{5,1},{6,2},{7,3},{8,12},{9,13},{10,... | collective-permute-start | bytes 786440 | tf_op jit(solution)/shard_map/ppermute | solution.py:258
  50.5 0.8 receive.20
  51.3 0.5 collective-permute-start.6
  51.8 7.7 %collective-permute-done.refs_0_ = bf16[1024,128]{1,0:T(8,128)(2,1)S(1)} collective-permute-done((bf16[1024,128]{1,0:T(8,128)(2,1)S(1)}, bf16[1024,128]{1,0:T(8,128)(2,1)S(1)}, u32[]{:S(2)}, u32[]{:S(2)}) %collective-permute-start) | collective-permute-done | bytes 262176 | tf_op jit(solution)/shard_map/ppermute | solution.py:258
  59.5 0.8 receive.21
  60.3 1.4 %collective-permute-start.5 = (bf16[1024,128]{1,0:T(8,128)(2,1)}, bf16[1024,128]{1,0:T(8,128)(2,1)S(1)}, u32[]{:S(2)}, u32[]{:S(2)}) collective-permute-start(bf16[1024,128]{1,0:T(8,128)(2,1)} %get-tuple-element.81), channel_id=1, source_target_pairs={{0,3},{1,2},{2,1},{3,0},{4,7},{5,6},{6,5},{7,4},{8,11},{9,10},{10,... | collective-permute-start | bytes 786440 | tf_op jit(solution)/shard_map/ppermute | solution.py:258
  61.7 0.8 receive.22
  62.5 2.4 %collective-permute-done.8.refs_0_ = bf16[1024,128]{1,0:T(8,128)(2,1)S(1)} collective-permute-done((bf16[1024,128]{1,0:T(8,128)(2,1)}, bf16[1024,128]{1,0:T(8,128)(2,1)S(1)}, u32[]{:S(2)}, u32[]{:S(2)}) %collective-permute-start.8) | collective-permute-done | bytes 262176 | tf_op jit(solution)/shard_map/ppermute | solution.py:258
  64.9 0.8 receive.23
  65.7 5.0 %collective-permute-done.7.refs_0_ = bf16[1024,128]{1,0:T(8,128)(2,1)S(1)} collective-permute-done((bf16[1024,128]{1,0:T(8,128)(2,1)}, bf16[1024,128]{1,0:T(8,128)(2,1)S(1)}, u32[]{:S(2)}, u32[]{:S(2)}) %collective-permute-start.7) | collective-permute-done | bytes 262176 | tf_op jit(solution)/shard_map/ppermute | solution.py:258
  70.7 0.8 receive.24
  71.5 2.3 %collective-permute-start.12 = (bf16[1024,128]{1,0:T(8,128)(2,1)}, bf16[1024,128]{1,0:T(8,128)(2,1)S(1)}, u32[]{:S(2)}, u32[]{:S(2)}) collective-permute-start(bf16[1024,128]{1,0:T(8,128)(2,1)} %get-tuple-element.103), channel_id=1, source_target_pairs={{0,11},{1,10},{2,9},{3,8},{4,15},{5,14},{6,13},{7,12},{8,3},{9,2},... | collective-permute-start | bytes 786440 | tf_op jit(solution)/shard_map/ppermute | solution.py:258
  73.8 2.7 %collective-permute-start.14 = (bf16[1024,128]{1,0:T(8,128)(2,1)S(1)}, bf16[1024,128]{1,0:T(8,128)(2,1)S(1)}, u32[]{:S(2)}, u32[]{:S(2)}) collective-permute-start(bf16[1024,128]{1,0:T(8,128)(2,1)S(1)} %copy-done.3), channel_id=1, source_target_pairs={{0,14},{1,15},{2,12},{3,13},{4,10},{5,11},{6,8},{7,9},{8,6},{9,7},... | collective-permute-start | bytes 786440 | tf_op jit(solution)/shard_map/ppermute | solution.py:258
  76.5 0.8 collective-permute-start.13
  77.3 16.4 %collective-permute-done.6.refs_0_ = bf16[1024,128]{1,0:T(8,128)(2,1)S(1)} collective-permute-done((bf16[1024,128]{1,0:T(8,128)(2,1)}, bf16[1024,128]{1,0:T(8,128)(2,1)S(1)}, u32[]{:S(2)}, u32[]{:S(2)}) %collective-permute-start.6) | collective-permute-done | bytes 262176 | tf_op jit(solution)/shard_map/ppermute | solution.py:258
  93.7 0.8 receive.25
  94.5 0.1 collective-permute-start.11
  94.6 0.8 receive.26
  95.4 2.5 %collective-permute-start.10 = (bf16[1024,128]{1,0:T(8,128)(2,1)}, bf16[1024,128]{1,0:T(8,128)(2,1)S(1)}, u32[]{:S(2)}, u32[]{:S(2)}) collective-permute-start(bf16[1024,128]{1,0:T(8,128)(2,1)} %get-tuple-element.101), channel_id=1, source_target_pairs={{0,15},{1,14},{2,13},{3,12},{4,11},{5,10},{6,9},{7,8},{8,7},{9,6},... | collective-permute-start | bytes 786440 | tf_op jit(solution)/shard_map/ppermute | solution.py:258
  98.0 0.8 receive.27
  98.8 1.4 %collective-permute-done.13.refs_0_ = bf16[1024,128]{1,0:T(8,128)(2,1)S(1)} collective-permute-done((bf16[1024,128]{1,0:T(8,128)(2,1)S(1)}, bf16[1024,128]{1,0:T(8,128)(2,1)S(1)}, u32[]{:S(2)}, u32[]{:S(2)}) %collective-permute-start.13) | collective-permute-done | bytes 262176 | tf_op jit(solution)/shard_map/ppermute | solution.py:258
  100.2 0.8 receive.28
  101.0 0.8 receive.29
  101.8 0.8 receive.30
  102.7 3.8 %collective-permute-done.10.refs_0_ = bf16[1024,128]{1,0:T(8,128)(2,1)S(1)} collective-permute-done((bf16[1024,128]{1,0:T(8,128)(2,1)}, bf16[1024,128]{1,0:T(8,128)(2,1)S(1)}, u32[]{:S(2)}, u32[]{:S(2)}) %collective-permute-start.10) | collective-permute-done | bytes 262176 | tf_op jit(solution)/shard_map/ppermute | solution.py:258
  106.5 0.8 receive.31
  107.3 0.1 reduce_sum.9
  107.4 0.1 reshape.9
  107.5 18.1 %all_to_all.11.sums = f32[16,1,128]{2,1,0:T(1,128)} all-to-all(f32[16,1,128]{2,1,0:T(1,128)S(1)} %broadcast_in_dim.8), channel_id=1, replica_groups=mesh['groups'=2,'sink'=16] {'sink'}, dimensions={0} | all-to-all | bytes 16384 | tf_op jit(solution)/shard_map/all_to_all | solution.py:287
  125.7 1.4 %finish.1 = f32[1,4,4]{2,1,0:T(4,128)} custom-call(s32[2,4]{1,0:T(2,128)} %bitcast.5, f32[16,1,128]{2,1,0:T(1,128)} %all_to_all.11.sums), custom_call_target="tpu_custom_call" | custom-call | tf_op jit(solution)/shard_map/finish/pallas_call | solution.py:244
  (16 shorter events, 0.0 us)
Async XLA Ops:
  16.2 19.8 %copy-start = (bf16[8,2,128,128]{3,2,1,0:T(8,128)(2,1)S(1)}, bf16[8,2,128,128]{3,2,1,0:T(8,128)(2,1)}, u32[]{:S(2)}) copy-start(bf16[8,2,128,128]{3,2,1,0:T(8,128)(2,1)} %refs_1_.31) | copy-start | bytes 1572868
  22.7 15.1 %collective-permute-start.4 = (bf16[1024,128]{1,0:T(8,128)(2,1)S(1)}, bf16[1024,128]{1,0:T(8,128)(2,1)S(1)}, u32[]{:S(2)}, u32[]{:S(2)}) collective-permute-start(bf16[1024,128]{1,0:T(8,128)(2,1)S(1)} %get-tuple-element.64), channel_id=1, source_target_pairs={{0,8},{1,9},{2,10},{3,11},{4,12},{5,13},{6,14},{7,15},{8,0},{9,1},... | collective-permute-start | bytes 786440 | tf_op jit(solution)/shard_map/ppermute | solution.py:258
  23.0 20.4 %collective-permute-start.3 = (bf16[1024,128]{1,0:T(8,128)(2,1)S(1)}, bf16[1024,128]{1,0:T(8,128)(2,1)S(1)}, u32[]{:S(2)}, u32[]{:S(2)}) collective-permute-start(bf16[1024,128]{1,0:T(8,128)(2,1)S(1)} %get-tuple-element.63), channel_id=1, source_target_pairs={{0,7},{1,6},{2,5},{3,4},{4,3},{5,2},{6,1},{7,0},{8,15},{9,14},{10,... | collective-permute-start | bytes 786440 | tf_op jit(solution)/shard_map/ppermute | solution.py:258
  23.6 22.3 %collective-permute-start.2 = (bf16[1024,128]{1,0:T(8,128)(2,1)S(1)}, bf16[1024,128]{1,0:T(8,128)(2,1)S(1)}, u32[]{:S(2)}, u32[]{:S(2)}) collective-permute-start(bf16[1024,128]{1,0:T(8,128)(2,1)S(1)} %get-tuple-element.62), channel_id=1, source_target_pairs={{0,12},{1,13},{2,14},{3,15},{4,8},{5,9},{6,10},{7,11},{8,4},{9,5},... | collective-permute-start | bytes 786440 | tf_op jit(solution)/shard_map/ppermute | solution.py:258
  26.1 24.4 %collective-permute-start.1 = (bf16[1024,128]{1,0:T(8,128)(2,1)S(1)}, bf16[1024,128]{1,0:T(8,128)(2,1)S(1)}, u32[]{:S(2)}, u32[]{:S(2)}) collective-permute-start(bf16[1024,128]{1,0:T(8,128)(2,1)S(1)} %get-tuple-element.61), channel_id=1, source_target_pairs={{0,6},{1,7},{2,4},{3,5},{4,2},{5,3},{6,0},{7,1},{8,14},{9,15},{10,... | collective-permute-start | bytes 786440 | tf_op jit(solution)/shard_map/ppermute | solution.py:258
  26.6 32.9 %collective-permute-start = (bf16[1024,128]{1,0:T(8,128)(2,1)S(1)}, bf16[1024,128]{1,0:T(8,128)(2,1)S(1)}, u32[]{:S(2)}, u32[]{:S(2)}) collective-permute-start(bf16[1024,128]{1,0:T(8,128)(2,1)S(1)} %get-tuple-element.60), channel_id=1, source_target_pairs={{0,9},{1,8},{2,11},{3,10},{4,13},{5,12},{6,15},{7,14},{8,1},{9,0},... | collective-permute-start | bytes 786440 | tf_op jit(solution)/shard_map/ppermute | solution.py:258
  36.0 1.0 copy-start.1
  38.6 23.1 %collective-permute-start.9 = (bf16[1024,128]{1,0:T(8,128)(2,1)}, bf16[1024,128]{1,0:T(8,128)(2,1)S(1)}, u32[]{:S(2)}, u32[]{:S(2)}) collective-permute-start(bf16[1024,128]{1,0:T(8,128)(2,1)} %get-tuple-element.85), channel_id=1, source_target_pairs={{0,5},{1,4},{2,7},{3,6},{4,1},{5,0},{6,3},{7,2},{8,13},{9,12},{10,... | collective-permute-start | bytes 786440 | tf_op jit(solution)/shard_map/ppermute | solution.py:258
  44.2 20.7 %collective-permute-start.8 = (bf16[1024,128]{1,0:T(8,128)(2,1)}, bf16[1024,128]{1,0:T(8,128)(2,1)S(1)}, u32[]{:S(2)}, u32[]{:S(2)}) collective-permute-start(bf16[1024,128]{1,0:T(8,128)(2,1)} %get-tuple-element.84), channel_id=1, source_target_pairs={{0,13},{1,12},{2,15},{3,14},{4,9},{5,8},{6,11},{7,10},{8,5},{9,4},... | collective-permute-start | bytes 786440 | tf_op jit(solution)/shard_map/ppermute | solution.py:258
  46.7 24.0 %collective-permute-start.7 = (bf16[1024,128]{1,0:T(8,128)(2,1)}, bf16[1024,128]{1,0:T(8,128)(2,1)S(1)}, u32[]{:S(2)}, u32[]{:S(2)}) collective-permute-start(bf16[1024,128]{1,0:T(8,128)(2,1)} %get-tuple-element.83), channel_id=1, source_target_pairs={{0,4},{1,5},{2,6},{3,7},{4,0},{5,1},{6,2},{7,3},{8,12},{9,13},{10,... | collective-permute-start | bytes 786440 | tf_op jit(solution)/shard_map/ppermute | solution.py:258
  51.3 42.4 %collective-permute-start.6 = (bf16[1024,128]{1,0:T(8,128)(2,1)}, bf16[1024,128]{1,0:T(8,128)(2,1)S(1)}, u32[]{:S(2)}, u32[]{:S(2)}) collective-permute-start(bf16[1024,128]{1,0:T(8,128)(2,1)} %get-tuple-element.82), channel_id=1, source_target_pairs={{0,10},{1,11},{2,8},{3,9},{4,14},{5,15},{6,12},{7,13},{8,2},{9,3},... | collective-permute-start | bytes 786440 | tf_op jit(solution)/shard_map/ppermute | solution.py:258
  60.3 34.3 %collective-permute-start.5 = (bf16[1024,128]{1,0:T(8,128)(2,1)}, bf16[1024,128]{1,0:T(8,128)(2,1)S(1)}, u32[]{:S(2)}, u32[]{:S(2)}) collective-permute-start(bf16[1024,128]{1,0:T(8,128)(2,1)} %get-tuple-element.81), channel_id=1, source_target_pairs={{0,3},{1,2},{2,1},{3,0},{4,7},{5,6},{6,5},{7,4},{8,11},{9,10},{10,... | collective-permute-start | bytes 786440 | tf_op jit(solution)/shard_map/ppermute | solution.py:258
  64.9 8.9 %copy-start.3 = (bf16[1024,128]{1,0:T(8,128)(2,1)S(1)}, bf16[1024,128]{1,0:T(8,128)(2,1)}, u32[]{:S(2)}) copy-start(bf16[1024,128]{1,0:T(8,128)(2,1)} %get-tuple-element.105) | copy-start | bytes 786436
  65.7 10.8 %copy-start.2 = (bf16[1024,128]{1,0:T(8,128)(2,1)S(1)}, bf16[1024,128]{1,0:T(8,128)(2,1)}, u32[]{:S(2)}) copy-start(bf16[1024,128]{1,0:T(8,128)(2,1)} %get-tuple-element.104) | copy-start | bytes 786436
  71.5 29.5 %collective-permute-start.12 = (bf16[1024,128]{1,0:T(8,128)(2,1)}, bf16[1024,128]{1,0:T(8,128)(2,1)S(1)}, u32[]{:S(2)}, u32[]{:S(2)}) collective-permute-start(bf16[1024,128]{1,0:T(8,128)(2,1)} %get-tuple-element.103), channel_id=1, source_target_pairs={{0,11},{1,10},{2,9},{3,8},{4,15},{5,14},{6,13},{7,12},{8,3},{9,2},... | collective-permute-start | bytes 786440 | tf_op jit(solution)/shard_map/ppermute | solution.py:258
  73.8 24.2 %collective-permute-start.14 = (bf16[1024,128]{1,0:T(8,128)(2,1)S(1)}, bf16[1024,128]{1,0:T(8,128)(2,1)S(1)}, u32[]{:S(2)}, u32[]{:S(2)}) collective-permute-start(bf16[1024,128]{1,0:T(8,128)(2,1)S(1)} %copy-done.3), channel_id=1, source_target_pairs={{0,14},{1,15},{2,12},{3,13},{4,10},{5,11},{6,8},{7,9},{8,6},{9,7},... | collective-permute-start | bytes 786440 | tf_op jit(solution)/shard_map/ppermute | solution.py:258
  76.5 23.6 %collective-permute-start.13 = (bf16[1024,128]{1,0:T(8,128)(2,1)S(1)}, bf16[1024,128]{1,0:T(8,128)(2,1)S(1)}, u32[]{:S(2)}, u32[]{:S(2)}) collective-permute-start(bf16[1024,128]{1,0:T(8,128)(2,1)S(1)} %copy-done.2), channel_id=1, source_target_pairs={{0,2},{1,3},{2,0},{3,1},{4,6},{5,7},{6,4},{7,5},{8,10},{9,11},{10,... | collective-permute-start | bytes 786440 | tf_op jit(solution)/shard_map/ppermute | solution.py:258
  94.5 7.3 %collective-permute-start.11 = (bf16[1024,128]{1,0:T(8,128)(2,1)}, bf16[1024,128]{1,0:T(8,128)(2,1)S(1)}, u32[]{:S(2)}, u32[]{:S(2)}) collective-permute-start(bf16[1024,128]{1,0:T(8,128)(2,1)} %get-tuple-element.102), channel_id=1, source_target_pairs={{0,1},{1,0},{2,3},{3,2},{4,5},{5,4},{6,7},{7,6},{8,9},{9,8},{10,11... | collective-permute-start | bytes 786440 | tf_op jit(solution)/shard_map/ppermute | solution.py:258
  95.4 11.1 %collective-permute-start.10 = (bf16[1024,128]{1,0:T(8,128)(2,1)}, bf16[1024,128]{1,0:T(8,128)(2,1)S(1)}, u32[]{:S(2)}, u32[]{:S(2)}) collective-permute-start(bf16[1024,128]{1,0:T(8,128)(2,1)} %get-tuple-element.101), channel_id=1, source_target_pairs={{0,15},{1,14},{2,13},{3,12},{4,11},{5,10},{6,9},{7,8},{8,7},{9,6},... | collective-permute-start | bytes 786440 | tf_op jit(solution)/shard_map/ppermute | solution.py:258

commit v3 on v2

--- a/solution.py
+++ b/solution.py
@@ -7,14 +7,14 @@
 
 NMOM = 4
 PITCH = 136
-GROUP = 16
+GROUP = 32
 F32 = jnp.float32
 BF16 = jnp.bfloat16
 IN_VMEM = pl.BlockSpec(memory_space=pltpu.VMEM)
 IN_SMEM = pl.BlockSpec(memory_space=pltpu.SMEM)
 IN_HBM = pl.BlockSpec(memory_space=pltpu.HBM)
 AHEAD = 5
-DEPTH = 4
+DEPTH = 2
 
 
 def in_hbm(array):
@@ -262,6 +262,7 @@
     far = list(range(devices // 2, devices))
     near = list(range(devices // 2 - 1, 0, -1))
     far = [d for pair in zip(far[: len(far) // 2], far[len(far) // 2 :]) for d in pair]
+    far[:2] = far[1::-1]
     sent = []
     for f, c in zip(far, near + [None]):
         sent += [f] if c is None else [f, c]

time: 127 us -> 126 us (level)
  starting transfers between devices: 22.4 us -> 16.7 us
  waiting for transfers between devices: 40.5 us -> 46 us
    ppermute x15, starting transfers between devices: 22.4 us -> 16.7 us  [send(): return lax.ppermute(message, 'sink', [(i, i ^ d) for i in range(devices)])]
    ppermute x15, waiting for transfers between devices: 40.5 us -> 46 us  [send(): return lax.ppermute(message, 'sink', [(i, i ^ d) for i in range(devices)])]
  transfers between devices with their start and end apart: 15 -> 15, of which waited for: 7 -> 10; matrix products, arithmetic and copies ran while one was open for 0% -> 0% of each run, Pallas kernels for 16% -> 16%
where the time goes in v3:
time: 126 us
  waiting for transfers between devices  46 us (37%)
  blocking collectives  32.1 us (25%)
  Pallas kernels  28.9 us (23%)
  starting transfers between devices  16.7 us (13%)
    ppermute x15, waiting for transfers between devices, send(): return lax.ppermute(message, 'sink', [(i, i ^ d) for i in range(devices)])  46 us
    all_to_all x1, blocking collectives, by_classes(): lax.all_to_all(jnp.broadcast_to(row, (devices, 1, width)), 'sink', split_...  17.6 us
    ppermute x15, starting transfers between devices, send(): return lax.ppermute(message, 'sink', [(i, i ^ d) for i in range(devices)])  16.7 us
    all_to_all x1, blocking collectives, by_classes(): lax.all_to_all(picked, 'sink', split_axis=0, concat_axis=0, tiled=True)  14.6 us
    pallas_call x2, Pallas kernels, contract(): pl.pallas_call(kernel, out_shape=[place(shape, BF16)] * count, in_specs=[...  13.4 us
    pallas_call x16, Pallas kernels, receive(): pl.pallas_call(kernel, out_shape=shapes, in_specs=specs, out_specs=places...  13 us
  transfers between devices with their start and end apart: 15, of which 10 were waited for; matrix products, arithmetic and copies ran while one was open for 0% of the time, Pallas kernels for 16%

profile of v3, /device:TPU:0, one launch (start us, length us, event | category | flops | bytes accessed | tf_op | source)
XLA Modules:
  0.0 125.8 jit_solution(4630349541757476642)
XLA Ops:
  0.6 1.0 pick.1
  1.6 14.6 %all_to_all.10.factors = bf16[16,3,8,128]{3,2,1,0:T(8,128)(2,1)S(1)} all-to-all(bf16[16,3,8,128]{3,2,1,0:T(8,128)(2,1)S(1)} %pick.1), channel_id=1, replica_groups=mesh['groups'=2,'sink'=16] {'sink'}, dimensions={0} | all-to-all | bytes 196608 | tf_op jit(solution)/shard_map/all_to_all | solution.py:261
  16.2 6.1 %contract.2 = (bf16[1024,128]{1,0:T(8,128)(2,1)S(1)}, bf16[1024,128]{1,0:T(8,128)(2,1)S(1)}, bf16[1024,128]{1,0:T(8,128)(2,1)S(1)}, bf16[1024,128]{1,0:T(8,128)(2,1)S(1)}, bf16[1024,128]{1,0:T(8,128)(2,1)S(1)}) custom-call(bf16[128,128,128]{2,1,0:T(8,128)(2,1)} %blocks.3, bf16[16,3,8,128]{3,2,1,0:T(8,128)(2,1)S(1)} %all_to_all.10.factors), custom_call_target="tpu_custom_call" | custom-call | tf_op jit(solution)/shard_map/contract/pallas_call | solution.py:131
  22.4 0.7 collective-permute-start.4
  23.1 2.6 %collective-permute-start.2 = (bf16[1024,128]{1,0:T(8,128)(2,1)S(1)}, bf16[1024,128]{1,0:T(8,128)(2,1)S(1)}, u32[]{:S(2)}, u32[]{:S(2)}) collective-permute-start(bf16[1024,128]{1,0:T(8,128)(2,1)S(1)} %get-tuple-element.62), channel_id=1, source_target_pairs={{0,8},{1,9},{2,10},{3,11},{4,12},{5,13},{6,14},{7,15},{8,0},{9,1},... | collective-permute-start | bytes 786440 | tf_op jit(solution)/shard_map/ppermute | solution.py:258
  25.7 0.6 collective-permute-start.1
  26.3 1.8 %collective-permute-start = (bf16[1024,128]{1,0:T(8,128)(2,1)S(1)}, bf16[1024,128]{1,0:T(8,128)(2,1)S(1)}, u32[]{:S(2)}, u32[]{:S(2)}) collective-permute-start(bf16[1024,128]{1,0:T(8,128)(2,1)S(1)} %get-tuple-element.60), channel_id=1, source_target_pairs={{0,9},{1,8},{2,11},{3,10},{4,13},{5,12},{6,15},{7,14},{8,1},{9,0},... | collective-permute-start | bytes 786440 | tf_op jit(solution)/shard_map/ppermute | solution.py:258
  28.1 7.3 %contract.3 = (bf16[1024,128]{1,0:T(8,128)(2,1)}, bf16[1024,128]{1,0:T(8,128)(2,1)}, bf16[1024,128]{1,0:T(8,128)(2,1)}, bf16[1024,128]{1,0:T(8,128)(2,1)}, bf16[...) custom-call(bf16[128,128,128]{2,1,0:T(8,128)(2,1)} %blocks.3, ...), custom_call_target="tpu_custom_call" | custom-call | tf_op jit(solution)/shard_map/contract/pallas_call | solution.py:131
  35.4 0.9 copy-done.1
  36.4 0.8 receive.16
  37.2 0.8 receive.17
  38.0 0.9 collective-permute-start.9
  38.9 0.7 collective-permute-done.3.refs_0_
  39.6 0.8 receive.18
  40.4 1.1 collective-permute-start.8
  41.5 6.6 %collective-permute-done.2.refs_0_ = bf16[1024,128]{1,0:T(8,128)(2,1)S(1)} collective-permute-done((bf16[1024,128]{1,0:T(8,128)(2,1)S(1)}, bf16[1024,128]{1,0:T(8,128)(2,1)S(1)}, u32[]{:S(2)}, u32[]{:S(2)}) %collective-permute-start.2) | collective-permute-done | bytes 262176 | tf_op jit(solution)/shard_map/ppermute | solution.py:258
  48.1 0.8 receive.19
  48.9 0.1 collective-permute-start.7
  49.0 1.8 %collective-permute-done.1.refs_0_ = bf16[1024,128]{1,0:T(8,128)(2,1)S(1)} collective-permute-done((bf16[1024,128]{1,0:T(8,128)(2,1)S(1)}, bf16[1024,128]{1,0:T(8,128)(2,1)S(1)}, u32[]{:S(2)}, u32[]{:S(2)}) %collective-permute-start.1) | collective-permute-done | bytes 262176 | tf_op jit(solution)/shard_map/ppermute | solution.py:258
  50.8 0.8 receive.20
  51.6 1.1 collective-permute-start.6
  52.7 5.2 %collective-permute-done.refs_0_ = bf16[1024,128]{1,0:T(8,128)(2,1)S(1)} collective-permute-done((bf16[1024,128]{1,0:T(8,128)(2,1)S(1)}, bf16[1024,128]{1,0:T(8,128)(2,1)S(1)}, u32[]{:S(2)}, u32[]{:S(2)}) %collective-permute-start) | collective-permute-done | bytes 262176 | tf_op jit(solution)/shard_map/ppermute | solution.py:258
  57.9 0.8 receive.21
  58.7 1.3 %collective-permute-start.5 = (bf16[1024,128]{1,0:T(8,128)(2,1)}, bf16[1024,128]{1,0:T(8,128)(2,1)S(1)}, u32[]{:S(2)}, u32[]{:S(2)}) collective-permute-start(bf16[1024,128]{1,0:T(8,128)(2,1)} %get-tuple-element.81), channel_id=1, source_target_pairs={{0,3},{1,2},{2,1},{3,0},{4,7},{5,6},{6,5},{7,4},{8,11},{9,10},{10,... | collective-permute-start | bytes 786440 | tf_op jit(solution)/shard_map/ppermute | solution.py:258
  60.1 1.2 collective-permute-done.9.refs_0_
  61.3 0.8 receive.22
  62.1 2.2 %collective-permute-done.8.refs_0_ = bf16[1024,128]{1,0:T(8,128)(2,1)S(1)} collective-permute-done((bf16[1024,128]{1,0:T(8,128)(2,1)}, bf16[1024,128]{1,0:T(8,128)(2,1)S(1)}, u32[]{:S(2)}, u32[]{:S(2)}) %collective-permute-start.8) | collective-permute-done | bytes 262176 | tf_op jit(solution)/shard_map/ppermute | solution.py:258
  64.3 0.8 receive.23
  65.1 7.8 %collective-permute-done.7.refs_0_ = bf16[1024,128]{1,0:T(8,128)(2,1)S(1)} collective-permute-done((bf16[1024,128]{1,0:T(8,128)(2,1)}, bf16[1024,128]{1,0:T(8,128)(2,1)S(1)}, u32[]{:S(2)}, u32[]{:S(2)}) %collective-permute-start.7) | collective-permute-done | bytes 262176 | tf_op jit(solution)/shard_map/ppermute | solution.py:258
  72.9 0.8 receive.24
  73.7 0.1 collective-permute-start.12
  73.8 2.1 %collective-permute-start.14 = (bf16[1024,128]{1,0:T(8,128)(2,1)S(1)}, bf16[1024,128]{1,0:T(8,128)(2,1)S(1)}, u32[]{:S(2)}, u32[]{:S(2)}) collective-permute-start(bf16[1024,128]{1,0:T(8,128)(2,1)S(1)} %copy-done.3), channel_id=1, source_target_pairs={{0,14},{1,15},{2,12},{3,13},{4,10},{5,11},{6,8},{7,9},{8,6},{9,7},... | collective-permute-start | bytes 786440 | tf_op jit(solution)/shard_map/ppermute | solution.py:258
  75.9 1.5 %collective-permute-start.13 = (bf16[1024,128]{1,0:T(8,128)(2,1)S(1)}, bf16[1024,128]{1,0:T(8,128)(2,1)S(1)}, u32[]{:S(2)}, u32[]{:S(2)}) collective-permute-start(bf16[1024,128]{1,0:T(8,128)(2,1)S(1)} %copy-done.2), channel_id=1, source_target_pairs={{0,2},{1,3},{2,0},{3,1},{4,6},{5,7},{6,4},{7,5},{8,10},{9,11},{10,... | collective-permute-start | bytes 786440 | tf_op jit(solution)/shard_map/ppermute | solution.py:258
  77.4 15.5 %collective-permute-done.6.refs_0_ = bf16[1024,128]{1,0:T(8,128)(2,1)S(1)} collective-permute-done((bf16[1024,128]{1,0:T(8,128)(2,1)}, bf16[1024,128]{1,0:T(8,128)(2,1)S(1)}, u32[]{:S(2)}, u32[]{:S(2)}) %collective-permute-start.6) | collective-permute-done | bytes 262176 | tf_op jit(solution)/shard_map/ppermute | solution.py:258
  93.0 0.8 receive.25
  93.9 0.8 receive.26
  94.7 2.7 %collective-permute-start.10 = (bf16[1024,128]{1,0:T(8,128)(2,1)}, bf16[1024,128]{1,0:T(8,128)(2,1)S(1)}, u32[]{:S(2)}, u32[]{:S(2)}) collective-permute-start(bf16[1024,128]{1,0:T(8,128)(2,1)} %get-tuple-element.101), channel_id=1, source_target_pairs={{0,15},{1,14},{2,13},{3,12},{4,11},{5,10},{6,9},{7,8},{8,7},{9,6},... | collective-permute-start | bytes 786440 | tf_op jit(solution)/shard_map/ppermute | solution.py:258
  97.5 0.8 receive.27
  98.3 0.9 collective-permute-done.13.refs_0_
  99.2 0.8 receive.28
  100.0 0.8 receive.29
  100.9 0.8 receive.30
  101.7 4.1 %collective-permute-done.10.refs_0_ = bf16[1024,128]{1,0:T(8,128)(2,1)S(1)} collective-permute-done((bf16[1024,128]{1,0:T(8,128)(2,1)}, bf16[1024,128]{1,0:T(8,128)(2,1)S(1)}, u32[]{:S(2)}, u32[]{:S(2)}) %collective-permute-start.10) | collective-permute-done | bytes 262176 | tf_op jit(solution)/shard_map/ppermute | solution.py:258
  105.8 0.8 receive.31
  106.6 0.1 reduce_sum.9
  106.7 0.1 reshape.9
  106.8 17.6 %all_to_all.11.sums = f32[16,1,128]{2,1,0:T(1,128)} all-to-all(f32[16,1,128]{2,1,0:T(1,128)S(1)} %broadcast_in_dim.8), channel_id=1, replica_groups=mesh['groups'=2,'sink'=16] {'sink'}, dimensions={0} | all-to-all | bytes 16384 | tf_op jit(solution)/shard_map/all_to_all | solution.py:288
  124.4 1.4 %finish.1 = f32[1,4,4]{2,1,0:T(4,128)} custom-call(s32[2,4]{1,0:T(2,128)} %bitcast.5, f32[16,1,128]{2,1,0:T(1,128)} %all_to_all.11.sums), custom_call_target="tpu_custom_call" | custom-call | tf_op jit(solution)/shard_map/finish/pallas_call | solution.py:244
  (16 shorter events, 0.1 us)
Async XLA Ops:
  16.2 19.2 %copy-start = (bf16[8,2,128,128]{3,2,1,0:T(8,128)(2,1)S(1)}, bf16[8,2,128,128]{3,2,1,0:T(8,128)(2,1)}, u32[]{:S(2)}) copy-start(bf16[8,2,128,128]{3,2,1,0:T(8,128)(2,1)} %refs_1_.31) | copy-start | bytes 1572868
  22.4 14.8 %collective-permute-start.4 = (bf16[1024,128]{1,0:T(8,128)(2,1)S(1)}, bf16[1024,128]{1,0:T(8,128)(2,1)S(1)}, u32[]{:S(2)}, u32[]{:S(2)}) collective-permute-start(bf16[1024,128]{1,0:T(8,128)(2,1)S(1)} %get-tuple-element.64), channel_id=1, source_target_pairs={{0,12},{1,13},{2,14},{3,15},{4,8},{5,9},{6,10},{7,11},{8,4},{9,5},... | collective-permute-start | bytes 786440 | tf_op jit(solution)/shard_map/ppermute | solution.py:258
  23.1 16.5 %collective-permute-start.3 = (bf16[1024,128]{1,0:T(8,128)(2,1)S(1)}, bf16[1024,128]{1,0:T(8,128)(2,1)S(1)}, u32[]{:S(2)}, u32[]{:S(2)}) collective-permute-start(bf16[1024,128]{1,0:T(8,128)(2,1)S(1)} %get-tuple-element.63), channel_id=1, source_target_pairs={{0,7},{1,6},{2,5},{3,4},{4,3},{5,2},{6,1},{7,0},{8,15},{9,14},{10,... | collective-permute-start | bytes 786440 | tf_op jit(solution)/shard_map/ppermute | solution.py:258
  23.1 25.0 %collective-permute-start.2 = (bf16[1024,128]{1,0:T(8,128)(2,1)S(1)}, bf16[1024,128]{1,0:T(8,128)(2,1)S(1)}, u32[]{:S(2)}, u32[]{:S(2)}) collective-permute-start(bf16[1024,128]{1,0:T(8,128)(2,1)S(1)} %get-tuple-element.62), channel_id=1, source_target_pairs={{0,8},{1,9},{2,10},{3,11},{4,12},{5,13},{6,14},{7,15},{8,0},{9,1},... | collective-permute-start | bytes 786440 | tf_op jit(solution)/shard_map/ppermute | solution.py:258
  25.7 25.1 %collective-permute-start.1 = (bf16[1024,128]{1,0:T(8,128)(2,1)S(1)}, bf16[1024,128]{1,0:T(8,128)(2,1)S(1)}, u32[]{:S(2)}, u32[]{:S(2)}) collective-permute-start(bf16[1024,128]{1,0:T(8,128)(2,1)S(1)} %get-tuple-element.61), channel_id=1, source_target_pairs={{0,6},{1,7},{2,4},{3,5},{4,2},{5,3},{6,0},{7,1},{8,14},{9,15},{10,... | collective-permute-start | bytes 786440 | tf_op jit(solution)/shard_map/ppermute | solution.py:258
  26.3 31.6 %collective-permute-start = (bf16[1024,128]{1,0:T(8,128)(2,1)S(1)}, bf16[1024,128]{1,0:T(8,128)(2,1)S(1)}, u32[]{:S(2)}, u32[]{:S(2)}) collective-permute-start(bf16[1024,128]{1,0:T(8,128)(2,1)S(1)} %get-tuple-element.60), channel_id=1, source_target_pairs={{0,9},{1,8},{2,11},{3,10},{4,13},{5,12},{6,15},{7,14},{8,1},{9,0},... | collective-permute-start | bytes 786440 | tf_op jit(solution)/shard_map/ppermute | solution.py:258
  35.4 1.0 copy-start.1
  38.0 23.3 %collective-permute-start.9 = (bf16[1024,128]{1,0:T(8,128)(2,1)}, bf16[1024,128]{1,0:T(8,128)(2,1)S(1)}, u32[]{:S(2)}, u32[]{:S(2)}) collective-permute-start(bf16[1024,128]{1,0:T(8,128)(2,1)} %get-tuple-element.85), channel_id=1, source_target_pairs={{0,5},{1,4},{2,7},{3,6},{4,1},{5,0},{6,3},{7,2},{8,13},{9,12},{10,... | collective-permute-start | bytes 786440 | tf_op jit(solution)/shard_map/ppermute | solution.py:258
  40.4 23.9 %collective-permute-start.8 = (bf16[1024,128]{1,0:T(8,128)(2,1)}, bf16[1024,128]{1,0:T(8,128)(2,1)S(1)}, u32[]{:S(2)}, u32[]{:S(2)}) collective-permute-start(bf16[1024,128]{1,0:T(8,128)(2,1)} %get-tuple-element.84), channel_id=1, source_target_pairs={{0,13},{1,12},{2,15},{3,14},{4,9},{5,8},{6,11},{7,10},{8,5},{9,4},... | collective-permute-start | bytes 786440 | tf_op jit(solution)/shard_map/ppermute | solution.py:258
  48.9 24.0 %collective-permute-start.7 = (bf16[1024,128]{1,0:T(8,128)(2,1)}, bf16[1024,128]{1,0:T(8,128)(2,1)S(1)}, u32[]{:S(2)}, u32[]{:S(2)}) collective-permute-start(bf16[1024,128]{1,0:T(8,128)(2,1)} %get-tuple-element.83), channel_id=1, source_target_pairs={{0,4},{1,5},{2,6},{3,7},{4,0},{5,1},{6,2},{7,3},{8,12},{9,13},{10,... | collective-permute-start | bytes 786440 | tf_op jit(solution)/shard_map/ppermute | solution.py:258
  51.6 41.4 %collective-permute-start.6 = (bf16[1024,128]{1,0:T(8,128)(2,1)}, bf16[1024,128]{1,0:T(8,128)(2,1)S(1)}, u32[]{:S(2)}, u32[]{:S(2)}) collective-permute-start(bf16[1024,128]{1,0:T(8,128)(2,1)} %get-tuple-element.82), channel_id=1, source_target_pairs={{0,10},{1,11},{2,8},{3,9},{4,14},{5,15},{6,12},{7,13},{8,2},{9,3},... | collective-permute-start | bytes 786440 | tf_op jit(solution)/shard_map/ppermute | solution.py:258
  58.7 35.2 %collective-permute-start.5 = (bf16[1024,128]{1,0:T(8,128)(2,1)}, bf16[1024,128]{1,0:T(8,128)(2,1)S(1)}, u32[]{:S(2)}, u32[]{:S(2)}) collective-permute-start(bf16[1024,128]{1,0:T(8,128)(2,1)} %get-tuple-element.81), channel_id=1, source_target_pairs={{0,3},{1,2},{2,1},{3,0},{4,7},{5,6},{6,5},{7,4},{8,11},{9,10},{10,... | collective-permute-start | bytes 786440 | tf_op jit(solution)/shard_map/ppermute | solution.py:258
  64.3 9.5 %copy-start.3 = (bf16[1024,128]{1,0:T(8,128)(2,1)S(1)}, bf16[1024,128]{1,0:T(8,128)(2,1)}, u32[]{:S(2)}) copy-start(bf16[1024,128]{1,0:T(8,128)(2,1)} %get-tuple-element.105) | copy-start | bytes 786436
  65.1 10.8 %copy-start.2 = (bf16[1024,128]{1,0:T(8,128)(2,1)S(1)}, bf16[1024,128]{1,0:T(8,128)(2,1)}, u32[]{:S(2)}) copy-start(bf16[1024,128]{1,0:T(8,128)(2,1)} %get-tuple-element.104) | copy-start | bytes 786436
  73.7 26.3 %collective-permute-start.12 = (bf16[1024,128]{1,0:T(8,128)(2,1)}, bf16[1024,128]{1,0:T(8,128)(2,1)S(1)}, u32[]{:S(2)}, u32[]{:S(2)}) collective-permute-start(bf16[1024,128]{1,0:T(8,128)(2,1)} %get-tuple-element.103), channel_id=1, source_target_pairs={{0,11},{1,10},{2,9},{3,8},{4,15},{5,14},{6,13},{7,12},{8,3},{9,2},... | collective-permute-start | bytes 786440 | tf_op jit(solution)/shard_map/ppermute | solution.py:258
  73.8 23.7 %collective-permute-start.14 = (bf16[1024,128]{1,0:T(8,128)(2,1)S(1)}, bf16[1024,128]{1,0:T(8,128)(2,1)S(1)}, u32[]{:S(2)}, u32[]{:S(2)}) collective-permute-start(bf16[1024,128]{1,0:T(8,128)(2,1)S(1)} %copy-done.3), channel_id=1, source_target_pairs={{0,14},{1,15},{2,12},{3,13},{4,10},{5,11},{6,8},{7,9},{8,6},{9,7},... | collective-permute-start | bytes 786440 | tf_op jit(solution)/shard_map/ppermute | solution.py:258
  75.9 23.3 %collective-permute-start.13 = (bf16[1024,128]{1,0:T(8,128)(2,1)S(1)}, bf16[1024,128]{1,0:T(8,128)(2,1)S(1)}, u32[]{:S(2)}, u32[]{:S(2)}) collective-permute-start(bf16[1024,128]{1,0:T(8,128)(2,1)S(1)} %copy-done.2), channel_id=1, source_target_pairs={{0,2},{1,3},{2,0},{3,1},{4,6},{5,7},{6,4},{7,5},{8,10},{9,11},{10,... | collective-permute-start | bytes 786440 | tf_op jit(solution)/shard_map/ppermute | solution.py:258
  93.8 7.0 %collective-permute-start.11 = (bf16[1024,128]{1,0:T(8,128)(2,1)}, bf16[1024,128]{1,0:T(8,128)(2,1)S(1)}, u32[]{:S(2)}, u32[]{:S(2)}) collective-permute-start(bf16[1024,128]{1,0:T(8,128)(2,1)} %get-tuple-element.102), channel_id=1, source_target_pairs={{0,1},{1,0},{2,3},{3,2},{4,5},{5,4},{6,7},{7,6},{8,9},{9,8},{10,11... | collective-permute-start | bytes 786440 | tf_op jit(solution)/shard_map/ppermute | solution.py:258
  94.7 11.1 %collective-permute-start.10 = (bf16[1024,128]{1,0:T(8,128)(2,1)}, bf16[1024,128]{1,0:T(8,128)(2,1)S(1)}, u32[]{:S(2)}, u32[]{:S(2)}) collective-permute-start(bf16[1024,128]{1,0:T(8,128)(2,1)} %get-tuple-element.101), channel_id=1, source_target_pairs={{0,15},{1,14},{2,13},{3,12},{4,11},{5,10},{6,9},{7,8},{8,7},{9,6},... | collective-permute-start | bytes 786440 | tf_op jit(solution)/shard_map/ppermute | solution.py:258

commit v4 on v3

--- a/solution.py
+++ b/solution.py
@@ -137,7 +137,7 @@
             pltpu.VMEM(blocks.shape, BF16),
             pltpu.VMEM((width, width), F32),
             pltpu.VMEM((2 * width, 2 * width), BF16),
-            pltpu.VMEM((width * PITCH, width), F32),
+            pltpu.VMEM((width * PITCH + width, width), F32),
             pltpu.SemaphoreType.DMA((steps * (1 + count) + 1,)),
         ]
         + [pltpu.VMEM(shape, BF16)] * (count if stored else 0),
@@ -176,7 +176,7 @@
         if 3 in aliases:
             sums[...] = refs[3][...]
         index = lax.axis_index("sink") ^ d
-        wide[...] = message[...].astype(F32)
+        wide[pl.ds(0, rows * width), :] = message[...].astype(F32)
         stores = []
         for r in range(rows):
             stage[r] = wide[pl.ds(r, width, stride=rows), :].astype(BF16)
@@ -197,7 +197,7 @@
         in_specs=specs,
         out_specs=places,
         scratch_shapes=[
-            pltpu.VMEM((rows * width, width), F32),
+            pltpu.VMEM((rows * width + rows, width), F32),
             pltpu.VMEM((rows, width, width), BF16),
             pltpu.SemaphoreType.DMA((rows,)),
         ],

time: 126 us -> 126 us (level)
  no operation moved by 1% of the time
where the time goes in v4:
time: 126 us
  waiting for transfers between devices  46 us (37%)
  blocking collectives  32.1 us (25%)
  Pallas kernels  28.9 us (23%)
  starting transfers between devices  16.7 us (13%)
    ppermute x15, waiting for transfers between devices, send(): return lax.ppermute(message, 'sink', [(i, i ^ d) for i in range(devices)])  46 us
    all_to_all x1, blocking collectives, by_classes(): lax.all_to_all(jnp.broadcast_to(row, (devices, 1, width)), 'sink', split_...  17.6 us
    ppermute x15, starting transfers between devices, send(): return lax.ppermute(message, 'sink', [(i, i ^ d) for i in range(devices)])  16.7 us
    all_to_all x1, blocking collectives, by_classes(): lax.all_to_all(picked, 'sink', split_axis=0, concat_axis=0, tiled=True)  14.6 us
    pallas_call x2, Pallas kernels, contract(): pl.pallas_call(kernel, out_shape=[place(shape, BF16)] * count, in_specs=[...  13.4 us
    pallas_call x16, Pallas kernels, receive(): pl.pallas_call(kernel, out_shape=shapes, in_specs=specs, out_specs=places...  13 us
  transfers between devices with their start and end apart: 15, of which 10 were waited for; matrix products, arithmetic and copies ran while one was open for 0% of the time, Pallas kernels for 16%

profile of v4, /device:TPU:0, one launch (start us, length us, event | category | flops | bytes accessed | tf_op | source)
XLA Modules:
  0.0 125.8 jit_solution(16585683638758708809)
XLA Ops:
  0.6 1.0 pick.1
  1.6 14.6 %all_to_all.10.factors = bf16[16,3,8,128]{3,2,1,0:T(8,128)(2,1)S(1)} all-to-all(bf16[16,3,8,128]{3,2,1,0:T(8,128)(2,1)S(1)} %pick.1), channel_id=1, replica_groups=mesh['groups'=2,'sink'=16] {'sink'}, dimensions={0} | all-to-all | bytes 196608 | tf_op jit(solution)/shard_map/all_to_all | solution.py:261
  16.2 6.1 %contract.2 = (bf16[1024,128]{1,0:T(8,128)(2,1)S(1)}, bf16[1024,128]{1,0:T(8,128)(2,1)S(1)}, bf16[1024,128]{1,0:T(8,128)(2,1)S(1)}, bf16[1024,128]{1,0:T(8,128)(2,1)S(1)}, bf16[1024,128]{1,0:T(8,128)(2,1)S(1)}) custom-call(bf16[128,128,128]{2,1,0:T(8,128)(2,1)} %blocks.3, bf16[16,3,8,128]{3,2,1,0:T(8,128)(2,1)S(1)} %all_to_all.10.factors), custom_call_target="tpu_custom_call" | custom-call | tf_op jit(solution)/shard_map/contract/pallas_call | solution.py:131
  22.4 0.7 collective-permute-start.4
  23.1 2.6 %collective-permute-start.2 = (bf16[1024,128]{1,0:T(8,128)(2,1)S(1)}, bf16[1024,128]{1,0:T(8,128)(2,1)S(1)}, u32[]{:S(2)}, u32[]{:S(2)}) collective-permute-start(bf16[1024,128]{1,0:T(8,128)(2,1)S(1)} %get-tuple-element.62), channel_id=1, source_target_pairs={{0,8},{1,9},{2,10},{3,11},{4,12},{5,13},{6,14},{7,15},{8,0},{9,1},... | collective-permute-start | bytes 786440 | tf_op jit(solution)/shard_map/ppermute | solution.py:258
  25.7 0.6 collective-permute-start.1
  26.3 1.8 %collective-permute-start = (bf16[1024,128]{1,0:T(8,128)(2,1)S(1)}, bf16[1024,128]{1,0:T(8,128)(2,1)S(1)}, u32[]{:S(2)}, u32[]{:S(2)}) collective-permute-start(bf16[1024,128]{1,0:T(8,128)(2,1)S(1)} %get-tuple-element.60), channel_id=1, source_target_pairs={{0,9},{1,8},{2,11},{3,10},{4,13},{5,12},{6,15},{7,14},{8,1},{9,0},... | collective-permute-start | bytes 786440 | tf_op jit(solution)/shard_map/ppermute | solution.py:258
  28.1 7.3 %contract.3 = (bf16[1024,128]{1,0:T(8,128)(2,1)}, bf16[1024,128]{1,0:T(8,128)(2,1)}, bf16[1024,128]{1,0:T(8,128)(2,1)}, bf16[1024,128]{1,0:T(8,128)(2,1)}, bf16[...) custom-call(bf16[128,128,128]{2,1,0:T(8,128)(2,1)} %blocks.3, ...), custom_call_target="tpu_custom_call" | custom-call | tf_op jit(solution)/shard_map/contract/pallas_call | solution.py:131
  35.4 0.9 copy-done.1
  36.4 0.8 receive.16
  37.2 0.8 receive.17
  38.0 0.9 collective-permute-start.9
  38.9 0.7 collective-permute-done.3.refs_0_
  39.6 0.8 receive.18
  40.4 1.1 collective-permute-start.8
  41.5 6.6 %collective-permute-done.2.refs_0_ = bf16[1024,128]{1,0:T(8,128)(2,1)S(1)} collective-permute-done((bf16[1024,128]{1,0:T(8,128)(2,1)S(1)}, bf16[1024,128]{1,0:T(8,128)(2,1)S(1)}, u32[]{:S(2)}, u32[]{:S(2)}) %collective-permute-start.2) | collective-permute-done | bytes 262176 | tf_op jit(solution)/shard_map/ppermute | solution.py:258
  48.1 0.8 receive.19
  48.9 0.1 collective-permute-start.7
  49.0 1.8 %collective-permute-done.1.refs_0_ = bf16[1024,128]{1,0:T(8,128)(2,1)S(1)} collective-permute-done((bf16[1024,128]{1,0:T(8,128)(2,1)S(1)}, bf16[1024,128]{1,0:T(8,128)(2,1)S(1)}, u32[]{:S(2)}, u32[]{:S(2)}) %collective-permute-start.1) | collective-permute-done | bytes 262176 | tf_op jit(solution)/shard_map/ppermute | solution.py:258
  50.8 0.8 receive.20
  51.6 1.1 collective-permute-start.6
  52.7 5.2 %collective-permute-done.refs_0_ = bf16[1024,128]{1,0:T(8,128)(2,1)S(1)} collective-permute-done((bf16[1024,128]{1,0:T(8,128)(2,1)S(1)}, bf16[1024,128]{1,0:T(8,128)(2,1)S(1)}, u32[]{:S(2)}, u32[]{:S(2)}) %collective-permute-start) | collective-permute-done | bytes 262176 | tf_op jit(solution)/shard_map/ppermute | solution.py:258
  57.9 0.8 receive.21
  58.7 1.3 %collective-permute-start.5 = (bf16[1024,128]{1,0:T(8,128)(2,1)}, bf16[1024,128]{1,0:T(8,128)(2,1)S(1)}, u32[]{:S(2)}, u32[]{:S(2)}) collective-permute-start(bf16[1024,128]{1,0:T(8,128)(2,1)} %get-tuple-element.81), channel_id=1, source_target_pairs={{0,3},{1,2},{2,1},{3,0},{4,7},{5,6},{6,5},{7,4},{8,11},{9,10},{10,... | collective-permute-start | bytes 786440 | tf_op jit(solution)/shard_map/ppermute | solution.py:258
  60.1 1.2 collective-permute-done.9.refs_0_
  61.3 0.8 receive.22
  62.1 2.2 %collective-permute-done.8.refs_0_ = bf16[1024,128]{1,0:T(8,128)(2,1)S(1)} collective-permute-done((bf16[1024,128]{1,0:T(8,128)(2,1)}, bf16[1024,128]{1,0:T(8,128)(2,1)S(1)}, u32[]{:S(2)}, u32[]{:S(2)}) %collective-permute-start.8) | collective-permute-done | bytes 262176 | tf_op jit(solution)/shard_map/ppermute | solution.py:258
  64.3 0.8 receive.23
  65.1 7.8 %collective-permute-done.7.refs_0_ = bf16[1024,128]{1,0:T(8,128)(2,1)S(1)} collective-permute-done((bf16[1024,128]{1,0:T(8,128)(2,1)}, bf16[1024,128]{1,0:T(8,128)(2,1)S(1)}, u32[]{:S(2)}, u32[]{:S(2)}) %collective-permute-start.7) | collective-permute-done | bytes 262176 | tf_op jit(solution)/shard_map/ppermute | solution.py:258
  72.9 0.8 receive.24
  73.7 0.1 collective-permute-start.12
  73.8 2.1 %collective-permute-start.14 = (bf16[1024,128]{1,0:T(8,128)(2,1)S(1)}, bf16[1024,128]{1,0:T(8,128)(2,1)S(1)}, u32[]{:S(2)}, u32[]{:S(2)}) collective-permute-start(bf16[1024,128]{1,0:T(8,128)(2,1)S(1)} %copy-done.3), channel_id=1, source_target_pairs={{0,14},{1,15},{2,12},{3,13},{4,10},{5,11},{6,8},{7,9},{8,6},{9,7},... | collective-permute-start | bytes 786440 | tf_op jit(solution)/shard_map/ppermute | solution.py:258
  75.9 1.5 %collective-permute-start.13 = (bf16[1024,128]{1,0:T(8,128)(2,1)S(1)}, bf16[1024,128]{1,0:T(8,128)(2,1)S(1)}, u32[]{:S(2)}, u32[]{:S(2)}) collective-permute-start(bf16[1024,128]{1,0:T(8,128)(2,1)S(1)} %copy-done.2), channel_id=1, source_target_pairs={{0,2},{1,3},{2,0},{3,1},{4,6},{5,7},{6,4},{7,5},{8,10},{9,11},{10,... | collective-permute-start | bytes 786440 | tf_op jit(solution)/shard_map/ppermute | solution.py:258
  77.4 15.5 %collective-permute-done.6.refs_0_ = bf16[1024,128]{1,0:T(8,128)(2,1)S(1)} collective-permute-done((bf16[1024,128]{1,0:T(8,128)(2,1)}, bf16[1024,128]{1,0:T(8,128)(2,1)S(1)}, u32[]{:S(2)}, u32[]{:S(2)}) %collective-permute-start.6) | collective-permute-done | bytes 262176 | tf_op jit(solution)/shard_map/ppermute | solution.py:258
  93.0 0.8 receive.25
  93.9 0.8 receive.26
  94.7 2.7 %collective-permute-start.10 = (bf16[1024,128]{1,0:T(8,128)(2,1)}, bf16[1024,128]{1,0:T(8,128)(2,1)S(1)}, u32[]{:S(2)}, u32[]{:S(2)}) collective-permute-start(bf16[1024,128]{1,0:T(8,128)(2,1)} %get-tuple-element.101), channel_id=1, source_target_pairs={{0,15},{1,14},{2,13},{3,12},{4,11},{5,10},{6,9},{7,8},{8,7},{9,6},... | collective-permute-start | bytes 786440 | tf_op jit(solution)/shard_map/ppermute | solution.py:258
  97.5 0.8 receive.27
  98.3 0.9 collective-permute-done.13.refs_0_
  99.2 0.8 receive.28
  100.0 0.8 receive.29
  100.9 0.8 receive.30
  101.7 4.1 %collective-permute-done.10.refs_0_ = bf16[1024,128]{1,0:T(8,128)(2,1)S(1)} collective-permute-done((bf16[1024,128]{1,0:T(8,128)(2,1)}, bf16[1024,128]{1,0:T(8,128)(2,1)S(1)}, u32[]{:S(2)}, u32[]{:S(2)}) %collective-permute-start.10) | collective-permute-done | bytes 262176 | tf_op jit(solution)/shard_map/ppermute | solution.py:258
  105.8 0.8 receive.31
  106.6 0.1 reduce_sum.9
  106.7 0.1 reshape.9
  106.8 17.6 %all_to_all.11.sums = f32[16,1,128]{2,1,0:T(1,128)} all-to-all(f32[16,1,128]{2,1,0:T(1,128)S(1)} %broadcast_in_dim.8), channel_id=1, replica_groups=mesh['groups'=2,'sink'=16] {'sink'}, dimensions={0} | all-to-all | bytes 16384 | tf_op jit(solution)/shard_map/all_to_all | solution.py:288
  124.4 1.4 %finish.1 = f32[1,4,4]{2,1,0:T(4,128)} custom-call(s32[2,4]{1,0:T(2,128)} %bitcast.5, f32[16,1,128]{2,1,0:T(1,128)} %all_to_all.11.sums), custom_call_target="tpu_custom_call" | custom-call | tf_op jit(solution)/shard_map/finish/pallas_call | solution.py:244
  (16 shorter events, 0.1 us)
Async XLA Ops:
  16.2 19.2 %copy-start = (bf16[8,2,128,128]{3,2,1,0:T(8,128)(2,1)S(1)}, bf16[8,2,128,128]{3,2,1,0:T(8,128)(2,1)}, u32[]{:S(2)}) copy-start(bf16[8,2,128,128]{3,2,1,0:T(8,128)(2,1)} %refs_1_.31) | copy-start | bytes 1572868
  22.4 14.8 %collective-permute-start.4 = (bf16[1024,128]{1,0:T(8,128)(2,1)S(1)}, bf16[1024,128]{1,0:T(8,128)(2,1)S(1)}, u32[]{:S(2)}, u32[]{:S(2)}) collective-permute-start(bf16[1024,128]{1,0:T(8,128)(2,1)S(1)} %get-tuple-element.64), channel_id=1, source_target_pairs={{0,12},{1,13},{2,14},{3,15},{4,8},{5,9},{6,10},{7,11},{8,4},{9,5},... | collective-permute-start | bytes 786440 | tf_op jit(solution)/shard_map/ppermute | solution.py:258
  23.1 16.5 %collective-permute-start.3 = (bf16[1024,128]{1,0:T(8,128)(2,1)S(1)}, bf16[1024,128]{1,0:T(8,128)(2,1)S(1)}, u32[]{:S(2)}, u32[]{:S(2)}) collective-permute-start(bf16[1024,128]{1,0:T(8,128)(2,1)S(1)} %get-tuple-element.63), channel_id=1, source_target_pairs={{0,7},{1,6},{2,5},{3,4},{4,3},{5,2},{6,1},{7,0},{8,15},{9,14},{10,... | collective-permute-start | bytes 786440 | tf_op jit(solution)/shard_map/ppermute | solution.py:258
  23.1 25.0 %collective-permute-start.2 = (bf16[1024,128]{1,0:T(8,128)(2,1)S(1)}, bf16[1024,128]{1,0:T(8,128)(2,1)S(1)}, u32[]{:S(2)}, u32[]{:S(2)}) collective-permute-start(bf16[1024,128]{1,0:T(8,128)(2,1)S(1)} %get-tuple-element.62), channel_id=1, source_target_pairs={{0,8},{1,9},{2,10},{3,11},{4,12},{5,13},{6,14},{7,15},{8,0},{9,1},... | collective-permute-start | bytes 786440 | tf_op jit(solution)/shard_map/ppermute | solution.py:258
  25.7 25.1 %collective-permute-start.1 = (bf16[1024,128]{1,0:T(8,128)(2,1)S(1)}, bf16[1024,128]{1,0:T(8,128)(2,1)S(1)}, u32[]{:S(2)}, u32[]{:S(2)}) collective-permute-start(bf16[1024,128]{1,0:T(8,128)(2,1)S(1)} %get-tuple-element.61), channel_id=1, source_target_pairs={{0,6},{1,7},{2,4},{3,5},{4,2},{5,3},{6,0},{7,1},{8,14},{9,15},{10,... | collective-permute-start | bytes 786440 | tf_op jit(solution)/shard_map/ppermute | solution.py:258
  26.3 31.6 %collective-permute-start = (bf16[1024,128]{1,0:T(8,128)(2,1)S(1)}, bf16[1024,128]{1,0:T(8,128)(2,1)S(1)}, u32[]{:S(2)}, u32[]{:S(2)}) collective-permute-start(bf16[1024,128]{1,0:T(8,128)(2,1)S(1)} %get-tuple-element.60), channel_id=1, source_target_pairs={{0,9},{1,8},{2,11},{3,10},{4,13},{5,12},{6,15},{7,14},{8,1},{9,0},... | collective-permute-start | bytes 786440 | tf_op jit(solution)/shard_map/ppermute | solution.py:258
  35.4 1.0 copy-start.1
  38.0 23.3 %collective-permute-start.9 = (bf16[1024,128]{1,0:T(8,128)(2,1)}, bf16[1024,128]{1,0:T(8,128)(2,1)S(1)}, u32[]{:S(2)}, u32[]{:S(2)}) collective-permute-start(bf16[1024,128]{1,0:T(8,128)(2,1)} %get-tuple-element.85), channel_id=1, source_target_pairs={{0,5},{1,4},{2,7},{3,6},{4,1},{5,0},{6,3},{7,2},{8,13},{9,12},{10,... | collective-permute-start | bytes 786440 | tf_op jit(solution)/shard_map/ppermute | solution.py:258
  40.4 23.9 %collective-permute-start.8 = (bf16[1024,128]{1,0:T(8,128)(2,1)}, bf16[1024,128]{1,0:T(8,128)(2,1)S(1)}, u32[]{:S(2)}, u32[]{:S(2)}) collective-permute-start(bf16[1024,128]{1,0:T(8,128)(2,1)} %get-tuple-element.84), channel_id=1, source_target_pairs={{0,13},{1,12},{2,15},{3,14},{4,9},{5,8},{6,11},{7,10},{8,5},{9,4},... | collective-permute-start | bytes 786440 | tf_op jit(solution)/shard_map/ppermute | solution.py:258
  48.9 24.0 %collective-permute-start.7 = (bf16[1024,128]{1,0:T(8,128)(2,1)}, bf16[1024,128]{1,0:T(8,128)(2,1)S(1)}, u32[]{:S(2)}, u32[]{:S(2)}) collective-permute-start(bf16[1024,128]{1,0:T(8,128)(2,1)} %get-tuple-element.83), channel_id=1, source_target_pairs={{0,4},{1,5},{2,6},{3,7},{4,0},{5,1},{6,2},{7,3},{8,12},{9,13},{10,... | collective-permute-start | bytes 786440 | tf_op jit(solution)/shard_map/ppermute | solution.py:258
  51.6 41.4 %collective-permute-start.6 = (bf16[1024,128]{1,0:T(8,128)(2,1)}, bf16[1024,128]{1,0:T(8,128)(2,1)S(1)}, u32[]{:S(2)}, u32[]{:S(2)}) collective-permute-start(bf16[1024,128]{1,0:T(8,128)(2,1)} %get-tuple-element.82), channel_id=1, source_target_pairs={{0,10},{1,11},{2,8},{3,9},{4,14},{5,15},{6,12},{7,13},{8,2},{9,3},... | collective-permute-start | bytes 786440 | tf_op jit(solution)/shard_map/ppermute | solution.py:258
  58.7 35.2 %collective-permute-start.5 = (bf16[1024,128]{1,0:T(8,128)(2,1)}, bf16[1024,128]{1,0:T(8,128)(2,1)S(1)}, u32[]{:S(2)}, u32[]{:S(2)}) collective-permute-start(bf16[1024,128]{1,0:T(8,128)(2,1)} %get-tuple-element.81), channel_id=1, source_target_pairs={{0,3},{1,2},{2,1},{3,0},{4,7},{5,6},{6,5},{7,4},{8,11},{9,10},{10,... | collective-permute-start | bytes 786440 | tf_op jit(solution)/shard_map/ppermute | solution.py:258
  64.3 9.5 %copy-start.3 = (bf16[1024,128]{1,0:T(8,128)(2,1)S(1)}, bf16[1024,128]{1,0:T(8,128)(2,1)}, u32[]{:S(2)}) copy-start(bf16[1024,128]{1,0:T(8,128)(2,1)} %get-tuple-element.105) | copy-start | bytes 786436
  65.1 10.8 %copy-start.2 = (bf16[1024,128]{1,0:T(8,128)(2,1)S(1)}, bf16[1024,128]{1,0:T(8,128)(2,1)}, u32[]{:S(2)}) copy-start(bf16[1024,128]{1,0:T(8,128)(2,1)} %get-tuple-element.104) | copy-start | bytes 786436
  73.7 26.3 %collective-permute-start.12 = (bf16[1024,128]{1,0:T(8,128)(2,1)}, bf16[1024,128]{1,0:T(8,128)(2,1)S(1)}, u32[]{:S(2)}, u32[]{:S(2)}) collective-permute-start(bf16[1024,128]{1,0:T(8,128)(2,1)} %get-tuple-element.103), channel_id=1, source_target_pairs={{0,11},{1,10},{2,9},{3,8},{4,15},{5,14},{6,13},{7,12},{8,3},{9,2},... | collective-permute-start | bytes 786440 | tf_op jit(solution)/shard_map/ppermute | solution.py:258
  73.8 23.7 %collective-permute-start.14 = (bf16[1024,128]{1,0:T(8,128)(2,1)S(1)}, bf16[1024,128]{1,0:T(8,128)(2,1)S(1)}, u32[]{:S(2)}, u32[]{:S(2)}) collective-permute-start(bf16[1024,128]{1,0:T(8,128)(2,1)S(1)} %copy-done.3), channel_id=1, source_target_pairs={{0,14},{1,15},{2,12},{3,13},{4,10},{5,11},{6,8},{7,9},{8,6},{9,7},... | collective-permute-start | bytes 786440 | tf_op jit(solution)/shard_map/ppermute | solution.py:258
  75.9 23.3 %collective-permute-start.13 = (bf16[1024,128]{1,0:T(8,128)(2,1)S(1)}, bf16[1024,128]{1,0:T(8,128)(2,1)S(1)}, u32[]{:S(2)}, u32[]{:S(2)}) collective-permute-start(bf16[1024,128]{1,0:T(8,128)(2,1)S(1)} %copy-done.2), channel_id=1, source_target_pairs={{0,2},{1,3},{2,0},{3,1},{4,6},{5,7},{6,4},{7,5},{8,10},{9,11},{10,... | collective-permute-start | bytes 786440 | tf_op jit(solution)/shard_map/ppermute | solution.py:258
  93.8 7.0 %collective-permute-start.11 = (bf16[1024,128]{1,0:T(8,128)(2,1)}, bf16[1024,128]{1,0:T(8,128)(2,1)S(1)}, u32[]{:S(2)}, u32[]{:S(2)}) collective-permute-start(bf16[1024,128]{1,0:T(8,128)(2,1)} %get-tuple-element.102), channel_id=1, source_target_pairs={{0,1},{1,0},{2,3},{3,2},{4,5},{5,4},{6,7},{7,6},{8,9},{9,8},{10,11... | collective-permute-start | bytes 786440 | tf_op jit(solution)/shard_map/ppermute | solution.py:258
  94.7 11.1 %collective-permute-start.10 = (bf16[1024,128]{1,0:T(8,128)(2,1)}, bf16[1024,128]{1,0:T(8,128)(2,1)S(1)}, u32[]{:S(2)}, u32[]{:S(2)}) collective-permute-start(bf16[1024,128]{1,0:T(8,128)(2,1)} %get-tuple-element.101), channel_id=1, source_target_pairs={{0,15},{1,14},{2,13},{3,12},{4,11},{5,10},{6,9},{7,8},{8,7},{9,6},... | collective-permute-start | bytes 786440 | tf_op jit(solution)/shard_map/ppermute | solution.py:258
